TPU v7x, 256 devices: a whole 4x4x8 slice. The times are simulated.
256 devices in a mesh: rep: 8 (over z_hi, core), fsdp: 16 (over y, x), tp: 2 (over z_lo).
Axes of the slice: x: 4, y: 4, z: 8 (z_hi: 4, z_lo: 2; z = z_hi * 2 + z_lo), core: 2. Of those that a mesh axis runs over, the one named last changes fastest.
Arguments:
- queries: bfloat16 [4, 512, 8192], P(None, ('rep', 'fsdp'), 'tp'), may hold values from -512 to 512
- cache_keys: bfloat16 [512, 1024, 512], P(('rep', 'fsdp'), None, 'tp'), may hold values from -5 to 5
- cache_values: bfloat16 [512, 1024, 512], P(('rep', 'fsdp'), None, 'tp'), may hold values from -6 to 6
- new_keys: bfloat16 [4, 512, 512], P(None, ('rep', 'fsdp'), 'tp'), may hold values from -6 to 6
- new_values: bfloat16 [4, 512, 512], P(None, ('rep', 'fsdp'), 'tp'), may hold values from -6 to 6
- lengths: int32 [512], P(('rep', 'fsdp')), may hold values from 64 to 1024, as said below
- attn_out_weight: bfloat16 [8192, 4096], P(('tp', 'rep'), 'fsdp'), may hold values from -0.125 to 0.125
- residual: bfloat16 [4, 512, 4096], P(None, 'rep', 'fsdp'), may hold values from -6 to 6
- norm_gain: float32 [4096], P('fsdp'), may hold values from 0.1 to 1.9
- expert_ids: int32 [4, 512, 8], P(None, 'rep'), may hold values from 0 to 15, all different within a row; in each aligned block of 64 rows (0 to 63, 64 to 127, ..., all dimensions but the last counted through in order) at most 48 rows name the same one
- gate_weights: bfloat16 [4, 512, 8], P(None, 'rep'), may hold values from 0.049804688 to 0.34960938
- expert_in: bfloat16 [16, 4096, 2, 1536], P('fsdp', 'rep', None, 'tp'), may hold values from -0.09375 to 0.09375
- expert_out: bfloat16 [16, 1536, 4096], P('fsdp', 'tp', 'rep'), may hold values from -0.15625 to 0.15625
Outputs:
- layer_out: bfloat16 [4, 512, 4096], P(None, 'rep', 'fsdp')
Inputs may be any that keep to these rules, and one draw needn't show every extreme that they name: `expert_ids`: each row names 8 different experts; in each aligned block of 64 rows (one step of one replica) no expert is named by more than 48 rows. `lengths`: some sequence has exactly 1024 filled positions.
All inputs are finite; a program needn't handle non-finite values.
Results may differ from a plain program's by a relative error of at most 0.0055.
Values may be sent and summed in bfloat16 or wider, within the bound.
No kernel may reach another device: no remote copies, remote signals or barrier semaphores. Data moves between devices by JAX's collectives and lax.ppermute only.
A program may use at most 128 MiB of HBM per device.

v0:
```python
import jax
import jax.numpy as jnp
from jax import lax
from jax.sharding import PartitionSpec as P

D = 4096
HD = 128


norm_eps = 1e-06


def attend_rows(queries, cache_keys, cache_values, new_keys, new_values, lengths):
    step_count, row_count, query_width = queries.shape
    cache_len = cache_keys.shape[1]
    kv_heads = cache_keys.shape[2] // HD
    group_size = query_width // (kv_heads * HD)
    query_heads = queries.reshape(step_count, row_count, kv_heads, group_size, HD)
    cache_heads = cache_keys.reshape(row_count, cache_len, kv_heads, HD)
    value_heads = cache_values.reshape(row_count, cache_len, kv_heads, HD)
    fresh_keys = new_keys.reshape(step_count, row_count, kv_heads, HD)
    fresh_values = new_values.reshape(step_count, row_count, kv_heads, HD)
    score_scale = HD ** (-0.5)
    cache_scores = (
        jnp.einsum(
            "srkgd,rpkd->srkgp", query_heads, cache_heads, preferred_element_type=jnp.float32
        )
        * score_scale
    )
    live_cache = jnp.arange(cache_len, dtype=jnp.int32)[None, :] < lengths[:, None]
    cache_scores = jnp.where(live_cache[None, :, None, None, :], cache_scores, -jnp.inf)
    fresh_scores = (
        jnp.einsum("srkgd,jrkd->srkgj", query_heads, fresh_keys, preferred_element_type=jnp.float32)
        * score_scale
    )
    step_index = jnp.arange(step_count, dtype=jnp.int32)
    causal = step_index[None, :] <= step_index[:, None]
    fresh_scores = jnp.where(causal[:, None, None, None, :], fresh_scores, -jnp.inf)
    row_max = jnp.maximum(jnp.max(cache_scores, axis=-1), jnp.max(fresh_scores, axis=-1))[..., None]
    cache_exp = jnp.exp(cache_scores - row_max)
    fresh_exp = jnp.exp(fresh_scores - row_max)
    row_total = jnp.sum(cache_exp, axis=-1, keepdims=True) + jnp.sum(
        fresh_exp, axis=-1, keepdims=True
    )
    cache_probs = (cache_exp / row_total).astype(jnp.bfloat16)
    fresh_probs = (fresh_exp / row_total).astype(jnp.bfloat16)
    combined = jnp.einsum(
        "srkgp,rpkd->srkgd", cache_probs, value_heads, preferred_element_type=jnp.float32
    )
    combined = combined + jnp.einsum(
        "srkgj,jrkd->srkgd", fresh_probs, fresh_values, preferred_element_type=jnp.float32
    )
    return combined.astype(jnp.bfloat16).reshape(step_count, row_count, query_width)


def on_device(
    queries,
    cache_keys,
    cache_values,
    new_keys,
    new_values,
    lengths,
    attn_out_weight,
    residual,
    norm_gain,
    expert_ids,
    gate_weights,
    expert_in,
    expert_out,
):
    attn = attend_rows(queries, cache_keys, cache_values, new_keys, new_values, lengths)
    out_rows = lax.all_gather(attn_out_weight, "rep", axis=0, tiled=True)
    partial_proj = jnp.einsum(
        "srh,hd->srd",
        lax.all_gather(attn, "fsdp", axis=1, tiled=True),
        out_rows,
        preferred_element_type=jnp.float32,
    )
    projected = lax.psum(partial_proj, "tp")
    attended = residual.astype(jnp.float32) + projected
    square_sums = lax.psum(jnp.sum(attended * attended, axis=-1), "fsdp")
    normed = (attended * lax.rsqrt(square_sums[..., None] / D + norm_eps) * norm_gain).astype(
        jnp.bfloat16
    )
    experts = lax.axis_size("fsdp")
    step_count, block_rows, top_count = expert_ids.shape
    capacity = 3 * attn.shape[1] * top_count // 2
    expert_range = jnp.arange(experts, dtype=jnp.int32)
    chosen = expert_ids[..., None] == expert_range
    onehot = jnp.sum(chosen.astype(jnp.int32), axis=2)
    slot_rank = jnp.cumsum(onehot, axis=1) - 1
    gate_pick = jnp.sum(
        jnp.where(chosen, gate_weights.astype(jnp.float32)[..., None], jnp.float32(0.0)), axis=2
    ).astype(jnp.bfloat16)
    slot_range = jnp.arange(capacity, dtype=jnp.int32)
    rank_by_expert = jnp.transpose(slot_rank, (0, 2, 1))
    hit_by_expert = jnp.transpose(onehot, (0, 2, 1))
    selector = (
        (rank_by_expert[:, :, None, :] == slot_range[None, None, :, None])
        & (hit_by_expert[:, :, None, :] > 0)
    ).astype(jnp.bfloat16)
    combiner = selector * jnp.transpose(gate_pick, (0, 2, 1))[:, :, None, :]
    dispatched = jnp.einsum(
        "secb,sbd->escd", selector, normed, preferred_element_type=jnp.float32
    ).astype(jnp.bfloat16)
    arrived = lax.all_to_all(dispatched, "fsdp", split_axis=0, concat_axis=3, tiled=True)
    model_width = arrived.shape[3]
    expert_rows = arrived.reshape(step_count * capacity, model_width)
    weight_in, weight_out = (
        lax.all_gather(expert_in, "rep", axis=1, tiled=True),
        lax.all_gather(expert_out, "rep", axis=2, tiled=True),
    )
    hidden_width = weight_in.shape[3]
    gate_up = jnp.dot(
        expert_rows,
        weight_in.reshape(model_width, 2 * hidden_width),
        preferred_element_type=jnp.float32,
    )
    hidden = (jax.nn.silu(gate_up[:, :hidden_width]) * gate_up[:, hidden_width:]).astype(
        jnp.bfloat16
    )
    expert_result = jnp.dot(hidden, weight_out[0], preferred_element_type=jnp.float32)
    column_width = model_width // experts
    summed = lax.psum(expert_result.reshape(1, step_count, capacity, experts, column_width), "tp")
    returned = lax.all_to_all(
        summed.astype(jnp.bfloat16), "fsdp", split_axis=3, concat_axis=0, tiled=True
    )
    returned = returned.reshape(experts, step_count, capacity, column_width)
    routed_sum = jnp.einsum(
        "secb,escd->sbd", combiner, returned, preferred_element_type=jnp.float32
    )
    layer_out = (attended + routed_sum).astype(jnp.bfloat16)
    return layer_out


def solution(mesh):
    placed = (
        P(None, ("rep", "fsdp"), "tp"),
        P(("rep", "fsdp"), None, "tp"),
        P(("rep", "fsdp"), None, "tp"),
        P(None, ("rep", "fsdp"), "tp"),
        P(None, ("rep", "fsdp"), "tp"),
        P(("rep", "fsdp")),
        P(("tp", "rep"), "fsdp"),
        P(None, "rep", "fsdp"),
        P("fsdp"),
        P(None, "rep", None),
        P(None, "rep", None),
        P("fsdp", "rep", None, "tp"),
        P("fsdp", "tp", "rep"),
    )
    return jax.shard_map(
        on_device, mesh=mesh, in_specs=placed, out_specs=P(None, "rep", "fsdp"), check_vma=False
    )
```

profile of v0, /device:TPU:32, one launch (start us, length us, event | category | flops | bytes accessed | tf_op | source)
XLA Modules:
  0.0 464.5 jit_solution(6565463752956911069)
XLA Ops:
  6.5 0.7 all-gather.7.cloned.1.call-update
  7.3 1.1 reshape.89
  8.4 4.1 reshape.88
  12.6 2.1 reshape.91
  15.2 2.5 bitcast_reduce_fusion
  17.8 0.6 fusion.8
  18.4 0.9 copy-done.2
  19.3 0.9 fusion.2
  20.5 0.7 reshape.107
  21.2 26.1 %all-gather.7.cloned.1.call-done = bf16[4096,256]{1,0:T(8,128)(2,1)} async-done(((bf16[512,256]{1,0:T(8,128)(2,1)}), bf16[4096,256]{1,0:T(8,128)(2,1)}) %all-gather.7.cloned.1.call-update) | async-done | bytes 2097168 | tf_op jit(solution)/shard_map/all_gather | solution.py:72
  47.3 51.5 %all-gather.5.cloned.1.call-done = bf16[4,64,4096]{2,0,1:T(4,128)(2,1)} async-done(((bf16[4,4,4096]{2,0,1:T(4,128)(2,1)}), bf16[4,64,4096]{2,0,1:T(4,128)(2,1)}) %all-gather.5.cloned.1.call-update) | async-done | bytes 2097168 | tf_op jit(solution)/shard_map/all_gather | solution.py:75
  98.9 5.3 %fusion = f32[4,64,256]{2,1,0:T(8,128)} fusion(bf16[4096,256]{1,0:T(8,128)(2,1)} %all-gather.7.cloned.1.call-done, bf16[4,64,4096]{2,0,1:T(4,128)(2,1)} %all-gather.5.cloned.1.call-done), kind=kOutput, calls=%fused_computation | convolution fusion | flops 536870912 | bytes 4456448 | tf_op jit(solution)/shard_map/srh,hd->srd/dot_general | solution.py:73
  104.3 0.5 all-gather.11.cloned.1.call-update
  104.9 0.5 all-gather.9.cloned.1.call-update
  105.8 31.7 %all-reduce.3.cloned.1.call-done = f32[4,64,256]{2,1,0:T(8,128)} async-done(((f32[4,64,256]{2,1,0:T(8,128)}), f32[4,64,256]{2,1,0:T(8,128)}) %all-reduce.3.cloned.1.call-update) | async-done | bytes 262160 | tf_op jit(solution)/shard_map/psum | solution.py:79
  137.5 1.1 multiply_reduce_fusion
  138.6 40.1 %psum.22 = f32[4,64]{1,0:T(4,128)S(1)} all-reduce(f32[4,64]{1,0:T(4,128)S(1)} %multiply_reduce_fusion), channel_id=1, replica_groups=mesh['rep'=8,'fsdp'=16,'tp'=2] {'fsdp'}, use_global_device_ids=true, to_apply=%region_9.10 | all-reduce | flops 256 | bytes 2048 | tf_op jit(solution)/shard_map/psum | solution.py:81
  178.6 1.6 fusion.15
  180.4 18.4 %all_to_all.30 = bf16[16,4,48,256]{3,2,1,0:T(8,128)(2,1)S(1)} all-to-all(bf16[16,4,48,256]{3,2,1,0:T(8,128)(2,1)S(1)} %copy.68), channel_id=1, replica_groups=mesh['rep'=8,'fsdp'=16,'tp'=2] {'fsdp'}, dimensions={0} | all-to-all | bytes 3145728 | tf_op jit(solution)/shard_map/all_to_all | solution.py:106
  198.8 0.9 copy.69
  199.7 0.7 copy.91
  200.4 9.5 %all-gather.11.cloned.1.call-done = bf16[1,768,4096]{2,1,0:T(8,128)(2,1)} async-done(((bf16[1,768,512]{2,1,0:T(8,128)(2,1)}), bf16[1,768,4096]{2,1,0:T(8,128)(2,1)}) %all-gather.11.cloned.1.call-update) | async-done | bytes 6291472 | tf_op jit(solution)/shard_map/all_gather | solution.py:111
  210.0 8.7 %copy.71 = bf16[4096,768]{1,0:T(8,128)(2,1)} copy(bf16[4096,768]{0,1:T(8,128)(2,1)} %bitcast.91) | data formatting | bytes 12582912 | tf_op jit(solution)/shard_map/dot_general | solution.py:122
  218.6 113.8 %all-gather.9.cloned.1.call-done = bf16[1,4096,2,768]{3,2,0,1:T(2,128)(2,1)} async-done(((bf16[1,512,2,768]{3,2,0,1:T(2,128)(2,1)}), bf16[1,4096,2,768]{3,2,0,1:T(2,128)(2,1)}) %all-gather.9.cloned.1.call-update) | async-done | bytes 12582928 | tf_op jit(solution)/shard_map/all_gather | solution.py:110
  332.4 9.1 %copy.92 = bf16[512,8,2,768]{3,1,2,0:T(8,128)(2,1)S(1)} copy(bf16[512,8,2,768]{3,2,1,0:T(2,128)(2,1)} %bitcast.89) | data formatting | bytes 25165824
  341.5 2.6 fusion.59
  344.3 3.8 convolution_bitcast_fusion
  348.1 77.0 %all-reduce.4 = bf16[1,4,48,16,256]{4,2,3,1,0:T(8,128)(2,1)S(1)} all-reduce(f32[1,4,48,16,256]{4,2,3,1,0:T(8,128)} %convolution_bitcast_fusion), channel_id=1, replica_groups=mesh['rep'=8,'fsdp'=16,'tp'=2] {'tp'}, use_global_device_ids=true, to_apply=%region_10.11 | all-reduce | flops 786432 | bytes 4718592 | tf_op jit(solution)/shard_map/psum | solution.py:124
  425.1 1.3 copy.72
  426.5 7.1 %all-to-all-start.1 = ((bf16[1,4,48,16,256]{4,2,1,0,3:T(8,128)(2,1)}), bf16[1,4,48,16,256]{4,2,1,0,3:T(8,128)(2,1)S(1)}, u32[]{:S(2)}, u32[]{:S(2)}) async-start(bf16[1,4,48,16,256]{4,2,1,0,3:T(8,128)(2,1)} %copy.72), calls=%async_computation.1 | async-start | bytes 3145728 | tf_op jit(solution)/shard_map/all_to_all | solution.py:125
  433.7 23.1 %all-to-all-done.1 = bf16[1,4,48,16,256]{4,2,1,0,3:T(8,128)(2,1)S(1)} async-done(((bf16[1,4,48,16,256]{4,2,1,0,3:T(8,128)(2,1)}), bf16[1,4,48,16,256]{4,2,1,0,3:T(8,128)(2,1)S(1)}, u32[]{:S(2)}, u32[]{:S(2)}) %all-to-all-start.1) | async-done | bytes 1572896 | tf_op jit(solution)/shard_map/all_to_all | solution.py:125
  456.8 1.2 fusion.24
  (49 shorter events, 1.9 us)
Async XLA Ops:
  6.5 40.8 %all-gather.7.cloned.1.call-start = ((), (), s32[]{:S(2)}) async-start(), calls=%async_computation.3 | async-start | bytes 2359296 | tf_op jit(solution)/shard_map/all_gather | solution.py:72
  7.3 91.6 %all-gather.5.cloned.1.call-start = ((), (), s32[]{:S(2)}) async-start(), calls=%async_computation.2 | async-start | bytes 2228224 | tf_op jit(solution)/shard_map/all_gather | solution.py:75
  8.4 4.2 copy-start.7
  8.4 4.2 copy-start.1
  12.5 2.1 copy-start.8
  12.5 2.1 copy-start.10
  17.7 1.6 copy-start.2
  21.2 116.3 %all-reduce.3.cloned.1.call-start = ((), (), s32[]{:S(2)}) async-start(), calls=%async_computation.4 | async-start | bytes 524288 | tf_op jit(solution)/shard_map/psum | solution.py:79
  104.2 1.2 copy-start.5
  104.2 33.3 %copy-start.4 = (bf16[4,64,256]{2,1,0:T(8,128)(2,1)S(1)}, bf16[4,64,256]{2,1,0:T(8,128)(2,1)}, u32[]{:S(2)}) copy-start(bf16[4,64,256]{2,1,0:T(8,128)(2,1)} %param.20) | copy-start | bytes 393220
  104.2 74.4 %copy-start.9 = (f32[256]{0:T(256)S(1)}, f32[256]{0:T(256)}, u32[]{:S(2)}) copy-start(f32[256]{0:T(256)} %param.21) | copy-start | bytes 3076
  104.2 105.7 %all-gather.11.cloned.1.call-start = ((), (), s32[]{:S(2)}) async-start(), calls=%async_computation.6 | async-start | bytes 7077888 | tf_op jit(solution)/shard_map/all_gather | solution.py:111
  104.8 227.6 %all-gather.9.cloned.1.call-start = ((), (), s32[]{:S(2)}) async-start(), calls=%async_computation.5 | async-start | bytes 14155776 | tf_op jit(solution)/shard_map/all_gather | solution.py:110
  341.5 2.8 copy-start
  426.5 7.1 %copy-start.6 = (bf16[4,64,8]{1,2,0:T(8,128)(2,1)S(1)}, bf16[4,64,8]{1,2,0:T(8,128)(2,1)}, u32[]{:S(2)}) copy-start(bf16[4,64,8]{1,2,0:T(8,128)(2,1)} %param.23) | copy-start | bytes 12292
  426.5 30.3 %copy-start.3 = (f32[4,64,256]{2,1,0:T(8,128)S(1)}, f32[4,64,256]{2,1,0:T(8,128)}, u32[]{:S(2)}) copy-start(f32[4,64,256]{2,1,0:T(8,128)} %all-reduce.3.cloned.1.call-done) | copy-start | bytes 786436
  426.5 30.3 %all-to-all-start.1 = ((bf16[1,4,48,16,256]{4,2,1,0,3:T(8,128)(2,1)}), bf16[1,4,48,16,256]{4,2,1,0,3:T(8,128)(2,1)S(1)}, u32[]{:S(2)}, u32[]{:S(2)}) async-start(bf16[1,4,48,16,256]{4,2,1,0,3:T(8,128)(2,1)} %copy.72), calls=%async_computation.1 | async-start | bytes 3145728 | tf_op jit(solution)/shard_map/all_to_all | solution.py:125
Sparse Core Ops, SparseCore 0:
  9.2 38.0 all-gather.6
  49.8 49.0 all-gather.4
  104.4 33.0 all-reduce.2
  139.3 70.6 all-gather.10
  211.8 120.5 all-gather.8
where the time goes:
time: 465 us
  waiting for transfers between devices  258 us (55%)
  blocking collectives  135 us (29%)
  local copies, waits for them, and re-layouts  29.9 us (6%)
  matrix products  18.6 us (4%)
  between operations  13.4 us (3%)
  starting transfers between devices  7.28 us (2%)
    all_gather x1, waiting for transfers between devices, on_device(): lax.all_gather(expert_in, 'rep', axis=1, tiled=True)  114 us
    psum x1, blocking collectives, on_device(): lax.psum(expert_result.reshape(1, step_count, capacity, experts, column_w...  77 us
    all_gather x1, waiting for transfers between devices, on_device(): lax.all_gather(attn, 'fsdp', axis=1, tiled=True)  51.5 us
    psum x1, blocking collectives, on_device(): square_sums = lax.psum(jnp.sum(attended * attended, axis=-1), 'fsdp')  40.1 us
    psum x1, waiting for transfers between devices, on_device(): projected = lax.psum(partial_proj, 'tp')  31.7 us
    all_gather x1, waiting for transfers between devices, on_device(): out_rows = lax.all_gather(attn_out_weight, 'rep', axis=0, tiled=True)  26.1 us
    all_to_all x1, waiting for transfers between devices, on_device(): lax.all_to_all(summed.astype(jnp.bfloat16), 'fsdp', split_axis=3, concat_...  23.1 us
    all_to_all x1, blocking collectives, on_device(): lax.all_to_all(dispatched, 'fsdp', split_axis=0, concat_axis=3, tiled=True)  18.4 us
  transfers between devices with their start and end apart: 6, of which 6 were waited for; matrix products, arithmetic and copies ran while one was open for 6% of the time, Pallas kernels for 0%

commit v1 on v0

v1 whole, which is shorter than its diff:
```python
import jax
import jax.numpy as jnp
from jax import lax
from jax.sharding import PartitionSpec as P

D = 4096
HD = 128


norm_eps = 1e-06


def attend_rows(queries, cache_keys, cache_values, new_keys, new_values, lengths):
    step_count, row_count, query_width = queries.shape
    cache_len = cache_keys.shape[1]
    kv_heads = cache_keys.shape[2] // HD
    group_size = query_width // (kv_heads * HD)
    query_heads = queries.reshape(step_count, row_count, kv_heads, group_size, HD)
    cache_heads = cache_keys.reshape(row_count, cache_len, kv_heads, HD)
    value_heads = cache_values.reshape(row_count, cache_len, kv_heads, HD)
    fresh_keys = new_keys.reshape(step_count, row_count, kv_heads, HD)
    fresh_values = new_values.reshape(step_count, row_count, kv_heads, HD)
    score_scale = HD ** (-0.5)
    cache_scores = (
        jnp.einsum(
            "srkgd,rpkd->srkgp", query_heads, cache_heads, preferred_element_type=jnp.float32
        )
        * score_scale
    )
    live_cache = jnp.arange(cache_len, dtype=jnp.int32)[None, :] < lengths[:, None]
    cache_scores = jnp.where(live_cache[None, :, None, None, :], cache_scores, -jnp.inf)
    fresh_scores = (
        jnp.einsum("srkgd,jrkd->srkgj", query_heads, fresh_keys, preferred_element_type=jnp.float32)
        * score_scale
    )
    step_index = jnp.arange(step_count, dtype=jnp.int32)
    causal = step_index[None, :] <= step_index[:, None]
    fresh_scores = jnp.where(causal[:, None, None, None, :], fresh_scores, -jnp.inf)
    row_max = jnp.maximum(jnp.max(cache_scores, axis=-1), jnp.max(fresh_scores, axis=-1))[..., None]
    cache_exp = jnp.exp(cache_scores - row_max)
    fresh_exp = jnp.exp(fresh_scores - row_max)
    row_total = jnp.sum(cache_exp, axis=-1, keepdims=True) + jnp.sum(
        fresh_exp, axis=-1, keepdims=True
    )
    cache_probs = (cache_exp / row_total).astype(jnp.bfloat16)
    fresh_probs = (fresh_exp / row_total).astype(jnp.bfloat16)
    combined = jnp.einsum(
        "srkgp,rpkd->srkgd", cache_probs, value_heads, preferred_element_type=jnp.float32
    )
    combined = combined + jnp.einsum(
        "srkgj,jrkd->srkgd", fresh_probs, fresh_values, preferred_element_type=jnp.float32
    )
    return combined.astype(jnp.bfloat16).reshape(step_count, row_count, query_width)


ZH, Y, X = 4, 4, 4
bf16 = jnp.bfloat16
f32 = jnp.float32


def across_chip():
    return [(r, r ^ 1) for r in range(2 * ZH)]


def along_z(d):
    return [(r, ((r // 2 + d) % ZH) * 2 + r % 2) for r in range(2 * ZH)]


def along_y(d):
    return [(f, ((f // X + d) % Y) * X + f % X) for f in range(Y * X)]


def along_x(d):
    return [(f, (f // X) * X + (f % X + d) % X) for f in range(Y * X)]


def swap_zy(other_half):
    pairs = []
    for z in range(ZH):
        for c in range(2):
            for y in range(Y):
                for x in range(X):
                    for t in range(2):
                        source = (((z * 2 + c) * Y + y) * X + x) * 2 + t
                        goal = (((y * 2 + c) * Y + z) * X + (x ^ (2 * c))) * 2 + (t ^ other_half)
                        pairs.append((source, goal))
    return pairs


ALL = ("rep", "fsdp", "tp")


def pieces_along(value, table):
    return jnp.stack([value] + [lax.ppermute(value, "fsdp", table(-d)) for d in range(1, 4)])


def unroll_first(value, shift):
    twice = jnp.concatenate([value, value], axis=0)
    return lax.dynamic_slice_in_dim(twice, value.shape[0] - shift, value.shape[0], axis=0)


def on_device(
    queries,
    cache_keys,
    cache_values,
    new_keys,
    new_values,
    lengths,
    attn_out_weight,
    residual,
    norm_gain,
    expert_ids,
    gate_weights,
    expert_in,
    expert_out,
):
    rep, fsdp = lax.axis_index("rep"), lax.axis_index("fsdp")
    z, c = rep // 2, rep % 2
    y, x = fsdp // X, fsdp % X
    steps, block, top = expert_ids.shape
    experts = Y * X
    cap = 48

    weight_pieces = [attn_out_weight] + [
        lax.ppermute(attn_out_weight, "rep", along_z(-d)) for d in range(1, ZH)
    ]
    mine = jnp.stack(weight_pieces)
    theirs = lax.ppermute(mine, "rep", across_chip())
    both = jnp.stack([jnp.where(c == 0, mine, theirs), jnp.where(c == 0, theirs, mine)], axis=1)
    out_rows = unroll_first(both, z).reshape(2 * ZH * attn_out_weight.shape[0], -1)

    near_in = expert_in[0].reshape(expert_in.shape[1], -1)
    far_in = lax.ppermute(near_in, "rep", across_chip())
    weight_out = lax.all_gather(expert_out[0], "rep", axis=0, tiled=False)

    swap_same, swap_cross = swap_zy(0), swap_zy(1)
    ids_there = lax.ppermute(expert_ids, ALL, swap_same)
    residual_there = lax.ppermute(residual, ALL, swap_same)
    gain_there = lax.ppermute(norm_gain, ALL, swap_same)

    slot_range = jnp.arange(cap, dtype=jnp.int32)

    def routing(ids):
        chosen = ids[..., None] == jnp.arange(experts, dtype=jnp.int32)
        onehot = jnp.sum(chosen.astype(jnp.int32), axis=2)
        rank = jnp.cumsum(onehot, axis=1) - 1
        rank = jnp.transpose(rank, (0, 2, 1))
        hit = jnp.transpose(onehot, (0, 2, 1)) > 0
        selector = (rank[:, :, None, :] == slot_range[None, None, :, None]) & hit[:, :, None, :]
        return chosen, selector.astype(bf16)

    _, selector_there = routing(ids_there)
    chosen, selector = routing(expert_ids)
    gate_pick = jnp.sum(
        jnp.where(chosen, gate_weights.astype(f32)[..., None], f32(0.0)), axis=2
    ).astype(bf16)
    combiner = selector * jnp.transpose(gate_pick, (0, 2, 1))[:, :, None, :]

    attn = attend_rows(queries, cache_keys, cache_values, new_keys, new_values, lengths)
    seqs, width = attn.shape[1], attn.shape[2]
    rows = attn.reshape(steps * seqs, width)
    first, second = rows[:, : width // 2], rows[:, width // 2 :]
    first = pieces_along(pieces_along(first, along_x), along_y)
    second = pieces_along(pieces_along(second, along_y), along_x)
    model = out_rows.shape[1]
    partial = jnp.dot(
        first.reshape(-1, width // 2), out_rows[: width // 2], preferred_element_type=f32
    ).reshape(Y, X, steps * seqs, model)
    partial = partial + jnp.swapaxes(
        jnp.dot(
            second.reshape(-1, width // 2), out_rows[width // 2 :], preferred_element_type=f32
        ).reshape(X, Y, steps * seqs, model),
        0,
        1,
    )
    partial = partial.astype(bf16)
    partial = unroll_first(partial, y)
    partial = jnp.swapaxes(unroll_first(jnp.swapaxes(partial, 0, 1), x), 0, 1)
    partial = jnp.transpose(
        partial.reshape(Y * X, steps, seqs, model), (1, 0, 2, 3)
    ).reshape(steps, block, model)

    there_same = lax.ppermute(partial, ALL, swap_same)
    there_cross = lax.ppermute(partial, ALL, swap_cross)
    here_cross = lax.ppermute(partial, "tp", [(0, 1), (1, 0)])

    attended_there = residual_there.astype(f32) + (
        there_same.astype(f32) + there_cross.astype(f32)
    )
    scaled = (attended_there * gain_there).astype(bf16)
    dispatched = jnp.einsum(
        "secb,sbd->escd", selector_there, scaled, preferred_element_type=f32
    ).astype(bf16)
    arrived = lax.all_to_all(
        dispatched.reshape(experts, steps * cap, model), "fsdp", split_axis=0, concat_axis=0, tiled=True
    ).reshape(ZH, 2, 2, steps * cap, model)

    attended = residual.astype(f32) + (partial.astype(f32) + here_cross.astype(f32))
    squares = jnp.sum(attended * attended, axis=-1)
    squares = jnp.sum(pieces_along(squares, along_x), axis=0)
    squares = jnp.sum(pieces_along(squares, along_y), axis=0)
    row_scale = lax.rsqrt(squares / D + norm_eps)
    own_selector = lax.dynamic_index_in_dim(selector, fsdp, axis=1, keepdims=False)
    slot_scale = jnp.sum(own_selector.astype(f32) * row_scale[:, None, :], axis=-1).reshape(
        steps * cap, 1
    )

    near_w = near_in.reshape(2, model, -1)
    far_w = far_in.reshape(2, model, -1)

    def gate_up_of(d):
        part = lax.dynamic_index_in_dim(arrived, (z + d) % ZH, axis=0, keepdims=False)
        total = sum(
            jnp.dot(part[i, j], w[j], preferred_element_type=f32)
            for i, w in enumerate((near_w, far_w))
            for j in range(2)
        )
        return total

    received = [
        lax.ppermute(gate_up_of(d).astype(bf16), "rep", along_z(d)) for d in range(1, ZH)
    ]
    gate_up = gate_up_of(0)
    for part in received:
        gate_up = gate_up + part.astype(f32)
    gate_up = gate_up * slot_scale
    half = gate_up.shape[1] // 2
    hidden = (jax.nn.silu(gate_up[:, :half]) * gate_up[:, half:]).astype(bf16)
    result = jnp.einsum("sh,rhd->rsd", hidden, weight_out, preferred_element_type=f32).astype(bf16)
    result = jnp.swapaxes(result.reshape(2 * ZH, steps * cap, 2, model), 1, 2)
    returned = lax.all_to_all(
        result.reshape(experts, steps * cap, model), "fsdp", split_axis=0, concat_axis=0, tiled=True
    ).reshape(experts, steps, cap, model)
    routed = jnp.einsum("secb,escd->sbd", combiner, returned, preferred_element_type=f32).astype(bf16)
    routed_cross = lax.ppermute(routed, "tp", [(0, 1), (1, 0)])
    return (attended + (routed.astype(f32) + routed_cross.astype(f32))).astype(bf16)


def solution(mesh):
    placed = (
        P(None, ("rep", "fsdp"), "tp"),
        P(("rep", "fsdp"), None, "tp"),
        P(("rep", "fsdp"), None, "tp"),
        P(None, ("rep", "fsdp"), "tp"),
        P(None, ("rep", "fsdp"), "tp"),
        P(("rep", "fsdp")),
        P(("tp", "rep"), "fsdp"),
        P(None, "rep", "fsdp"),
        P("fsdp"),
        P(None, "rep", None),
        P(None, "rep", None),
        P("fsdp", "rep", None, "tp"),
        P("fsdp", "tp", "rep"),
    )
    return jax.shard_map(
        on_device, mesh=mesh, in_specs=placed, out_specs=P(None, "rep", "fsdp"), check_vma=False
    )
```

time: 465 us -> 305 us (0.66)
  waiting for transfers between devices: 258 us -> 110 us
  blocking collectives: 135 us -> 0 us
  starting transfers between devices: 7.28 us -> 119 us
  other arithmetic: 2.25 us -> 17.2 us
  local copies, waits for them, and re-layouts: 29.9 us -> 23.8 us
    all_gather x4 -> x1, waiting for transfers between devices: 201 us -> 0.02 us  [on_device(): weight_out = lax.all_gather(expert_out[0], 'rep', axis=0, tiled=False)]
    psum x2 -> x0, blocking collectives: 117 us -> none  [the longest x1 77 us: on_device(): lax.psum(expert_result.reshape(1, step_count, capacity, experts, column_w...]
    ppermute x0 -> x33, waiting for transfers between devices: none -> 91.5 us  [the longest x3 34.1 us: on_device(): lax.ppermute(gate_up_of(d).astype(bf16), 'rep', along_z(d))]
    ppermute x0 -> x33, starting transfers between devices: none -> 81.7 us  [the longest x18 44.3 us: pieces_along(): lax.ppermute(value, 'fsdp', table(-d))]
    psum x1 -> x0, waiting for transfers between devices: 31.7 us -> none  [on_device(): projected = lax.psum(partial_proj, 'tp')]
    all_to_all x1 -> x2, starting transfers between devices: 7.11 us -> 37.4 us  [the longest x1 22.2 us: on_device(): lax.all_to_all(dispatched.reshape(experts, steps * cap, model), 'fsdp', s...]
    all_to_all x1 -> x0, blocking collectives: 18.4 us -> none  [on_device(): lax.all_to_all(dispatched, 'fsdp', split_axis=0, concat_axis=3, tiled=True)]
    dot_general x1 -> x0, local copies, waits for them, and re-layouts: 8.65 us -> none  [on_device(): jnp.dot(hidden, weight_out[0], preferred_element_type=jnp.float32)]
  transfers between devices with their start and end apart: 6 -> 36, of which waited for: 6 -> 15; matrix products, arithmetic and copies ran while one was open for 6% -> 17% of each run, Pallas kernels for 0% -> 0%
where the time goes in v1:
time: 305 us; the launch traced here: 303 us
  starting transfers between devices  119 us (39%)
  waiting for transfers between devices  110 us (36%)
  local copies, waits for them, and re-layouts  23.8 us (8%)
  matrix products  18.9 us (6%)
  other arithmetic  17.2 us (6%)
  between operations  14 us (5%)
    ppermute x18, starting transfers between devices, pieces_along(): lax.ppermute(value, 'fsdp', table(-d))  44.3 us
    ppermute x3, waiting for transfers between devices, on_device(): lax.ppermute(gate_up_of(d).astype(bf16), 'rep', along_z(d))  34.1 us
    ppermute x3, waiting for transfers between devices, on_device(): lax.ppermute(attn_out_weight, 'rep', along_z(-d))  22.8 us
    ppermute x18, waiting for transfers between devices, pieces_along(): lax.ppermute(value, 'fsdp', table(-d))  22.4 us
    all_to_all x1, starting transfers between devices, on_device(): lax.all_to_all(dispatched.reshape(experts, steps * cap, model), 'fsdp', s...  22.2 us
    all_to_all x1, waiting for transfers between devices, on_device(): lax.all_to_all(result.reshape(experts, steps * cap, model), 'fsdp', split...  18.3 us
    all_to_all x1, starting transfers between devices, on_device(): lax.all_to_all(result.reshape(experts, steps * cap, model), 'fsdp', split...  15.2 us
    ppermute x1, starting transfers between devices, on_device(): routed_cross = lax.ppermute(routed, 'tp', [(0, 1), (1, 0)])  9.38 us
  transfers between devices with their start and end apart: 36, of which 15 were waited for; matrix products, arithmetic and copies ran while one was open for 17% of the time, Pallas kernels for 0%

profile of v1, /device:TPU:32, one launch (start us, length us, event | category | flops | bytes accessed | tf_op | source)
XLA Modules:
  0.0 302.8 jit_solution(14040172838869685034)
XLA Ops:
  6.5 5.4 %collective-permute-start.6 = (bf16[512,256]{1,0:T(8,128)(2,1)}, bf16[512,256]{1,0:T(8,128)(2,1)S(1)}, u32[]{:S(2)}, u32[]{:S(2)}) collective-permute-start(bf16[512,256]{1,0:T(8,128)(2,1)} %param.19), channel_id=1, source_target_pairs={{0,192},{32,224},{64,0},{96,32},{128,64},{160,96},{192,128},{224,1... | collective-permute-start | bytes 786440 | tf_op jit(solution)/shard_map/ppermute | solution.py:125
  13.4 2.4 collective-permute-start.8
  17.6 4.0 %reshape.140 = bf16[4,1024,2,128]{3,2,1,0:T(2,128)(2,1)} reshape(bf16[4,1024,256]{2,1,0:T(8,128)(2,1)} %param.14) | data formatting | bytes 4194304 | tf_op jit(solution)/shard_map/reshape | solution.py:19
  21.6 2.5 bitcast_reduce_fusion
  26.2 4.1 %reshape.143 = bf16[4,1024,2,128]{3,2,1,0:T(2,128)(2,1)} reshape(bf16[4,1024,256]{2,1,0:T(8,128)(2,1)} %param.15) | data formatting | bytes 4194304 | tf_op jit(solution)/shard_map/reshape | solution.py:20
  30.3 3.1 %fusion.14 = f32[4,2,4,16,128]{4,3,2,1,0:T(8,128)S(1)} fusion(bf16[4,1024,2,128,1]{3,2,1,0,4:T(2,128)(2,1)} %bitcast.198, f32[4,2,1024,4,16]{2,4,3,1,0:T(8,128)} %copy-done.2, f32[4,4,2,16]{3,0,2,1:T(4,128)S(1)} %add.155, f32[4,4,2,16]{3,0,2,1:T(4,128)S(1)} %max.7, pred[4,1024]{1,0:T(4,128)(4,1)S(1)} %iota_compare_fusion.4), kind=kOutput, calls=%fused_computation.26 | convolution fusion | flops 136839168 | bytes 4464640 | tf_op jit(solution)/shard_map/srkgp,rpkd->srkgd/dot_general | solution.py:47
  33.8 7.0 %collective-permute-done.7 = bf16[512,256]{1,0:T(8,128)(2,1)S(1)} collective-permute-done((bf16[512,256]{1,0:T(8,128)(2,1)}, bf16[512,256]{1,0:T(8,128)(2,1)S(1)}, u32[]{:S(2)}, u32[]{:S(2)}) %collective-permute-start.7) | collective-permute-done | bytes 262176 | tf_op jit(solution)/shard_map/ppermute | solution.py:125
  40.9 15.8 %collective-permute-done.8 = bf16[512,256]{1,0:T(8,128)(2,1)S(1)} collective-permute-done((bf16[512,256]{1,0:T(8,128)(2,1)}, bf16[512,256]{1,0:T(8,128)(2,1)S(1)}, u32[]{:S(2)}, u32[]{:S(2)}) %collective-permute-start.8) | collective-permute-done | bytes 262176 | tf_op jit(solution)/shard_map/ppermute | solution.py:125
  59.2 2.2 collective-permute-start.10
  73.7 1.9 collective-permute-start
  77.2 2.1 collective-permute-start.17
  80.3 1.9 collective-permute-start.20
  89.0 15.7 %collective-permute-start.3 = (bf16[4,16,2048]{2,1,0:T(8,128)(2,1)S(1)}, bf16[4,16,2048]{2,1,0:T(8,128)(2,1)S(1)}, u32[]{:S(2)}, u32[]{:S(2)}) collective-permute-start(bf16[4,16,2048]{2,1,0:T(8,128)(2,1)S(1)} %get-tuple-element.18), channel_id=1, source_target_pairs={{0,24},{2,26},{4,28},{6,30},{8,0},{10,2},{12,4},{14,6},{16,8},{18,... | collective-permute-start | bytes 786440 | tf_op jit(solution)/shard_map/ppermute | solution.py:94
  104.7 6.8 %collective-permute-start.4 = (bf16[4,16,2048]{2,1,0:T(8,128)(2,1)S(1)}, bf16[4,16,2048]{2,1,0:T(8,128)(2,1)S(1)}, u32[]{:S(2)}, u32[]{:S(2)}) collective-permute-start(bf16[4,16,2048]{2,1,0:T(8,128)(2,1)S(1)} %get-tuple-element.18), channel_id=1, source_target_pairs={{0,16},{2,18},{4,20},{6,22},{8,24},{10,26},{12,28},{14,30},{16,0},... | collective-permute-start | bytes 786440 | tf_op jit(solution)/shard_map/ppermute | solution.py:94
  112.0 5.1 %collective-permute-start.22 = (bf16[512,1536]{1,0:T(8,128)(2,1)}, bf16[512,1536]{1,0:T(8,128)(2,1)S(1)}, u32[]{:S(2)}, u32[]{:S(2)}) collective-permute-start(bf16[512,1536]{1,0:T(8,128)(2,1)} %bitcast.96), channel_id=1, source_target_pairs={{0,32},{32,0},{64,96},{96,64},{128,160},{160,128},{192,224},{224,1... | collective-permute-start | bytes 4718600 | tf_op jit(solution)/shard_map/ppermute | solution.py:133
  118.6 5.7 %collective-permute-done.5 = bf16[4,16,2048]{2,1,0:T(8,128)(2,1)S(1)} collective-permute-done((bf16[4,16,2048]{2,1,0:T(8,128)(2,1)S(1)}, bf16[4,16,2048]{2,1,0:T(8,128)(2,1)S(1)}, u32[]{:S(2)}, u32[]{:S(2)}) %collective-permute-start.5) | collective-permute-done | bytes 262176 | tf_op jit(solution)/shard_map/ppermute | solution.py:94
  127.3 4.2 %collective-permute-done.19 = bf16[4,64,256]{2,1,0:T(8,128)(2,1)} collective-permute-done((bf16[4,64,256]{2,1,0:T(8,128)(2,1)S(1)}, bf16[4,64,256]{2,1,0:T(8,128)(2,1)}, u32[]{:S(2)}, u32[]{:S(2)}) %collective-permute-start.19) | collective-permute-done | bytes 131104 | tf_op jit(solution)/shard_map/ppermute | solution.py:184
  134.4 22.2 %all-to-all-start = ((bf16[16,192,256]{2,1,0:T(8,128)(2,1)}), bf16[16,192,256]{2,1,0:T(8,128)(2,1)}, u32[]{:S(2)}, u32[]{:S(2)}) async-start(bf16[16,192,256]{2,1,0:T(8,128)(2,1)} %bitcast.195), calls=%async_computation | async-start | bytes 3145728 | tf_op jit(solution)/shard_map/all_to_all | solution.py:194
  157.4 2.3 fusion.110
  161.0 5.0 %collective-permute-done.16 = bf16[4,64,256]{2,1,0:T(8,128)(2,1)S(1)} collective-permute-done((bf16[4,64,256]{2,1,0:T(8,128)(2,1)S(1)}, bf16[4,64,256]{2,1,0:T(8,128)(2,1)S(1)}, u32[]{:S(2)}, u32[]{:S(2)}) %collective-permute-start.16) | collective-permute-done | bytes 131104 | tf_op jit(solution)/shard_map/ppermute | solution.py:185
  166.1 3.2 %collective-permute-start.26 = (f32[4,64]{1,0:T(4,128)S(1)}, f32[4,64]{1,0:T(4,128)S(1)}, u32[]{:S(2)}, u32[]{:S(2)}) collective-permute-start(f32[4,64]{1,0:T(4,128)S(1)} %multiply_reduce_fusion), channel_id=1, source_target_pairs={{0,6},{2,0},{4,2},{6,4},{8,14},{10,8},{12,10},{14,12},{16,22},{18,... | collective-permute-start | bytes 3080 | tf_op jit(solution)/shard_map/ppermute | solution.py:94
  171.0 10.0 %collective-permute-done.26 = f32[4,64]{1,0:T(4,128)S(1)} collective-permute-done((f32[4,64]{1,0:T(4,128)S(1)}, f32[4,64]{1,0:T(4,128)S(1)}, u32[]{:S(2)}, u32[]{:S(2)}) %collective-permute-start.26) | collective-permute-done | bytes 1056 | tf_op jit(solution)/shard_map/ppermute | solution.py:94
  181.0 2.2 collective-permute-done.27
  199.9 4.5 %collective-permute-start.24 = (bf16[192,1536]{1,0:T(8,128)(2,1)S(1)}, bf16[192,1536]{1,0:T(8,128)(2,1)S(1)}, u32[]{:S(2)}, u32[]{:S(2)}) collective-permute-start(bf16[192,1536]{1,0:T(8,128)(2,1)S(1)} %fusion.9), channel_id=1, source_target_pairs={{0,128},{32,160},{64,192},{96,224},{128,0},{160,32},{192,64},{224,... | collective-permute-start | bytes 1769480 | tf_op jit(solution)/shard_map/ppermute | solution.py:221
  205.7 1.8 collective-permute-start.25
  208.5 32.1 %collective-permute-done.23 = bf16[192,1536]{1,0:T(8,128)(2,1)S(1)} collective-permute-done((bf16[192,1536]{1,0:T(8,128)(2,1)S(1)}, bf16[192,1536]{1,0:T(8,128)(2,1)S(1)}, u32[]{:S(2)}, u32[]{:S(2)}) %collective-permute-start.23) | collective-permute-done | bytes 589856 | tf_op jit(solution)/shard_map/ppermute | solution.py:221
  240.5 2.0 collective-permute-done.25
  243.1 4.2 %fusion.25 = bf16[8,192,512]{2,1,0:T(8,128)(2,1)S(1)} fusion(bf16[8,768,512]{2,1,0:T(8,128)(2,1)} %all-gather.2.cloned.1.call-done, f32[192,1536]{1,0:T(8,128)S(1)} %fusion.7), kind=kOutput, calls=%fused_computation.45 | convolution fusion | flops 1209630720 | bytes 9043968 | tf_op jit(solution)/shard_map/sh,rhd->rsd/dot_general | solution.py:229
  248.8 15.2 %all-to-all-start.1 = ((bf16[16,192,256]{2,1,0:T(8,128)(2,1)}), bf16[16,192,256]{2,1,0:T(8,128)(2,1)S(1)}, u32[]{:S(2)}, u32[]{:S(2)}) async-start(bf16[16,192,256]{2,1,0:T(8,128)(2,1)} %bitcast.74), calls=%async_computation.1 | async-start | bytes 3145728 | tf_op jit(solution)/shard_map/all_to_all | solution.py:231
  264.1 18.3 %all-to-all-done.1 = bf16[16,192,256]{2,1,0:T(8,128)(2,1)S(1)} async-done(((bf16[16,192,256]{2,1,0:T(8,128)(2,1)}), bf16[16,192,256]{2,1,0:T(8,128)(2,1)S(1)}, u32[]{:S(2)}, u32[]{:S(2)}) %all-to-all-start.1) | async-done | bytes 1572896 | tf_op jit(solution)/shard_map/all_to_all | solution.py:231
  282.9 9.4 %collective-permute-start.32 = (bf16[4,64,256]{2,1,0:T(8,128)(2,1)S(1)}, bf16[4,64,256]{2,1,0:T(8,128)(2,1)S(1)}, u32[]{:S(2)}, u32[]{:S(2)}) collective-permute-start(bf16[4,64,256]{2,1,0:T(8,128)(2,1)S(1)} %fusion.34), channel_id=1, source_target_pairs={{0,1},{1,0},{2,3},{3,2},{4,5},{5,4},{6,7},{7,6},{8,9},{9,8},{10,11... | collective-permute-start | bytes 393224 | tf_op jit(solution)/shard_map/ppermute | solution.py:235
  292.3 2.9 collective-permute-done.32
  (158 shorter events, 63.6 us)
Async XLA Ops:
  6.5 236.6 %all-gather.2.cloned.1.call-start = ((), (), s32[]{:S(2)}) async-start(), calls=%async_computation.2 | async-start | bytes 7077888 | tf_op jit(solution)/shard_map/all_gather | solution.py:134
  6.5 27.3 %collective-permute-start.6 = (bf16[512,256]{1,0:T(8,128)(2,1)}, bf16[512,256]{1,0:T(8,128)(2,1)S(1)}, u32[]{:S(2)}, u32[]{:S(2)}) collective-permute-start(bf16[512,256]{1,0:T(8,128)(2,1)} %param.19), channel_id=1, source_target_pairs={{0,192},{32,224},{64,0},{96,32},{128,64},{160,96},{192,128},{224,1... | collective-permute-start | bytes 786440 | tf_op jit(solution)/shard_map/ppermute | solution.py:125
  11.9 28.9 %collective-permute-start.7 = (bf16[512,256]{1,0:T(8,128)(2,1)}, bf16[512,256]{1,0:T(8,128)(2,1)S(1)}, u32[]{:S(2)}, u32[]{:S(2)}) collective-permute-start(bf16[512,256]{1,0:T(8,128)(2,1)} %param.19), channel_id=1, source_target_pairs={{0,128},{32,160},{64,192},{96,224},{128,0},{160,32},{192,64},{224,... | collective-permute-start | bytes 786440 | tf_op jit(solution)/shard_map/ppermute | solution.py:125
  13.4 43.2 %collective-permute-start.8 = (bf16[512,256]{1,0:T(8,128)(2,1)}, bf16[512,256]{1,0:T(8,128)(2,1)S(1)}, u32[]{:S(2)}, u32[]{:S(2)}) collective-permute-start(bf16[512,256]{1,0:T(8,128)(2,1)} %param.19), channel_id=1, source_target_pairs={{0,64},{32,96},{64,128},{96,160},{128,192},{160,224},{192,0},{224,... | collective-permute-start | bytes 786440 | tf_op jit(solution)/shard_map/ppermute | solution.py:125
  58.5 27.2 %collective-permute-start.9 = (bf16[4,512,256]{2,1,0:T(8,128)(2,1)}, bf16[4,512,256]{2,1,0:T(8,128)(2,1)S(1)}, u32[]{:S(2)}, u32[]{:S(2)}) collective-permute-start(bf16[4,512,256]{2,1,0:T(8,128)(2,1)} %pad_maximum_fusion.1), channel_id=1, source_target_pairs={{0,32},{32,0},{64,96},{96,64},{128,160},{160,128},{192,224},{224,1... | collective-permute-start | bytes 3145736 | tf_op jit(solution)/shard_map/ppermute | solution.py:128
  59.2 14.4 %collective-permute-start.10 = (bf16[16,2048]{1,0:T(8,128)(2,1)}, bf16[16,2048]{1,0:T(8,128)(2,1)}, u32[]{:S(2)}, u32[]{:S(2)}) collective-permute-start(bf16[16,2048]{1,0:T(8,128)(2,1)} %get-tuple-element.23), channel_id=1, source_target_pairs={{0,24},{2,26},{4,28},{6,30},{8,0},{10,2},{12,4},{14,6},{16,8},{18,... | collective-permute-start | bytes 196616 | tf_op jit(solution)/shard_map/ppermute | solution.py:94
  61.4 14.2 %collective-permute-start.11 = (bf16[16,2048]{1,0:T(8,128)(2,1)}, bf16[16,2048]{1,0:T(8,128)(2,1)}, u32[]{:S(2)}, u32[]{:S(2)}) collective-permute-start(bf16[16,2048]{1,0:T(8,128)(2,1)} %get-tuple-element.23), channel_id=1, source_target_pairs={{0,16},{2,18},{4,20},{6,22},{8,24},{10,26},{12,28},{14,30},{16,0},... | collective-permute-start | bytes 196616 | tf_op jit(solution)/shard_map/ppermute | solution.py:94
  62.6 14.6 %collective-permute-start.12 = (bf16[16,2048]{1,0:T(8,128)(2,1)}, bf16[16,2048]{1,0:T(8,128)(2,1)}, u32[]{:S(2)}, u32[]{:S(2)}) collective-permute-start(bf16[16,2048]{1,0:T(8,128)(2,1)} %get-tuple-element.23), channel_id=1, source_target_pairs={{0,8},{2,10},{4,12},{6,14},{8,16},{10,18},{12,20},{14,22},{16,24},... | collective-permute-start | bytes 196616 | tf_op jit(solution)/shard_map/ppermute | solution.py:94
  68.3 12.0 %collective-permute-start.2 = (bf16[16,2048]{1,0:T(8,128)(2,1)}, bf16[16,2048]{1,0:T(8,128)(2,1)}, u32[]{:S(2)}, u32[]{:S(2)}) collective-permute-start(bf16[16,2048]{1,0:T(8,128)(2,1)} %get-tuple-element.24), channel_id=1, source_target_pairs={{0,2},{2,4},{4,6},{6,0},{8,10},{10,12},{12,14},{14,8},{16,18},{18,... | collective-permute-start | bytes 196616 | tf_op jit(solution)/shard_map/ppermute | solution.py:94
  73.7 8.5 %collective-permute-start = (bf16[16,2048]{1,0:T(8,128)(2,1)}, bf16[16,2048]{1,0:T(8,128)(2,1)S(1)}, u32[]{:S(2)}, u32[]{:S(2)}) collective-permute-start(bf16[16,2048]{1,0:T(8,128)(2,1)} %get-tuple-element.24), channel_id=1, source_target_pairs={{0,6},{2,0},{4,2},{6,4},{8,14},{10,8},{12,10},{14,12},{16,22},{18,... | collective-permute-start | bytes 196616 | tf_op jit(solution)/shard_map/ppermute | solution.py:94
  75.6 7.9 %collective-permute-start.1 = (bf16[16,2048]{1,0:T(8,128)(2,1)}, bf16[16,2048]{1,0:T(8,128)(2,1)S(1)}, u32[]{:S(2)}, u32[]{:S(2)}) collective-permute-start(bf16[16,2048]{1,0:T(8,128)(2,1)} %get-tuple-element.24), channel_id=1, source_target_pairs={{0,4},{2,6},{4,0},{6,2},{8,12},{10,14},{12,8},{14,10},{16,20},{18,... | collective-permute-start | bytes 196616 | tf_op jit(solution)/shard_map/ppermute | solution.py:94
  77.2 50.1 %collective-permute-start.17 = (bf16[4,64,256]{2,1,0:T(8,128)(2,1)}, bf16[4,64,256]{2,1,0:T(8,128)(2,1)}, u32[]{:S(2)}, u32[]{:S(2)}) collective-permute-start(bf16[4,64,256]{2,1,0:T(8,128)(2,1)} %param.20), channel_id=1, source_target_pairs={{0,0},{1,1},{2,2},{3,3},{4,4},{5,5},{6,6},{7,7},{8,64},{9,65},{10,... | collective-permute-start | bytes 393224 | tf_op jit(solution)/shard_map/ppermute | solution.py:138
  80.3 47.0 %collective-permute-start.20 = (f32[256]{0:T(256)}, f32[256]{0:T(256)}, u32[]{:S(2)}, u32[]{:S(2)}) collective-permute-start(f32[256]{0:T(256)} %param.21), channel_id=1, source_target_pairs={{0,0},{1,1},{2,2},{3,3},{4,4},{5,5},{6,6},{7,7},{8,64},{9,65},{10,... | collective-permute-start | bytes 3080 | tf_op jit(solution)/shard_map/ppermute | solution.py:139
  82.2 6.8 %collective-permute-start.13 = (bf16[4,16,2048]{2,1,0:T(8,128)(2,1)S(1)}, bf16[4,16,2048]{2,1,0:T(8,128)(2,1)S(1)}, u32[]{:S(2)}, u32[]{:S(2)}) collective-permute-start(bf16[4,16,2048]{2,1,0:T(8,128)(2,1)S(1)} %get-tuple-element.20), channel_id=1, source_target_pairs={{0,6},{2,0},{4,2},{6,4},{8,14},{10,8},{12,10},{14,12},{16,22},{18,... | collective-permute-start | bytes 786440 | tf_op jit(solution)/shard_map/ppermute | solution.py:94
  83.5 21.2 %collective-permute-start.14 = (bf16[4,16,2048]{2,1,0:T(8,128)(2,1)S(1)}, bf16[4,16,2048]{2,1,0:T(8,128)(2,1)S(1)}, u32[]{:S(2)}, u32[]{:S(2)}) collective-permute-start(bf16[4,16,2048]{2,1,0:T(8,128)(2,1)S(1)} %get-tuple-element.20), channel_id=1, source_target_pairs={{0,4},{2,6},{4,0},{6,2},{8,12},{10,14},{12,8},{14,10},{16,20},{18,... | collective-permute-start | bytes 786440 | tf_op jit(solution)/shard_map/ppermute | solution.py:94
  85.7 25.8 %collective-permute-start.15 = (bf16[4,16,2048]{2,1,0:T(8,128)(2,1)S(1)}, bf16[4,16,2048]{2,1,0:T(8,128)(2,1)S(1)}, u32[]{:S(2)}, u32[]{:S(2)}) collective-permute-start(bf16[4,16,2048]{2,1,0:T(8,128)(2,1)S(1)} %get-tuple-element.20), channel_id=1, source_target_pairs={{0,2},{2,4},{4,6},{6,0},{8,10},{10,12},{12,14},{14,8},{16,18},{18,... | collective-permute-start | bytes 786440 | tf_op jit(solution)/shard_map/ppermute | solution.py:94
  89.0 23.0 %collective-permute-start.3 = (bf16[4,16,2048]{2,1,0:T(8,128)(2,1)S(1)}, bf16[4,16,2048]{2,1,0:T(8,128)(2,1)S(1)}, u32[]{:S(2)}, u32[]{:S(2)}) collective-permute-start(bf16[4,16,2048]{2,1,0:T(8,128)(2,1)S(1)} %get-tuple-element.18), channel_id=1, source_target_pairs={{0,24},{2,26},{4,28},{6,30},{8,0},{10,2},{12,4},{14,6},{16,8},{18,... | collective-permute-start | bytes 786440 | tf_op jit(solution)/shard_map/ppermute | solution.py:94
  104.7 13.9 %collective-permute-start.4 = (bf16[4,16,2048]{2,1,0:T(8,128)(2,1)S(1)}, bf16[4,16,2048]{2,1,0:T(8,128)(2,1)S(1)}, u32[]{:S(2)}, u32[]{:S(2)}) collective-permute-start(bf16[4,16,2048]{2,1,0:T(8,128)(2,1)S(1)} %get-tuple-element.18), channel_id=1, source_target_pairs={{0,16},{2,18},{4,20},{6,22},{8,24},{10,26},{12,28},{14,30},{16,0},... | collective-permute-start | bytes 786440 | tf_op jit(solution)/shard_map/ppermute | solution.py:94
  111.6 12.8 %collective-permute-start.5 = (bf16[4,16,2048]{2,1,0:T(8,128)(2,1)S(1)}, bf16[4,16,2048]{2,1,0:T(8,128)(2,1)S(1)}, u32[]{:S(2)}, u32[]{:S(2)}) collective-permute-start(bf16[4,16,2048]{2,1,0:T(8,128)(2,1)S(1)} %get-tuple-element.18), channel_id=1, source_target_pairs={{0,8},{2,10},{4,12},{6,14},{8,16},{10,18},{12,20},{14,22},{16,24},... | collective-permute-start | bytes 786440 | tf_op jit(solution)/shard_map/ppermute | solution.py:94
  112.0 84.8 %collective-permute-start.22 = (bf16[512,1536]{1,0:T(8,128)(2,1)}, bf16[512,1536]{1,0:T(8,128)(2,1)S(1)}, u32[]{:S(2)}, u32[]{:S(2)}) collective-permute-start(bf16[512,1536]{1,0:T(8,128)(2,1)} %bitcast.96), channel_id=1, source_target_pairs={{0,32},{32,0},{64,96},{96,64},{128,160},{160,128},{192,224},{224,1... | collective-permute-start | bytes 4718600 | tf_op jit(solution)/shard_map/ppermute | solution.py:133
  134.4 60.6 %all-to-all-start = ((bf16[16,192,256]{2,1,0:T(8,128)(2,1)}), bf16[16,192,256]{2,1,0:T(8,128)(2,1)}, u32[]{:S(2)}, u32[]{:S(2)}) async-start(bf16[16,192,256]{2,1,0:T(8,128)(2,1)} %bitcast.195), calls=%async_computation | async-start | bytes 3145728 | tf_op jit(solution)/shard_map/all_to_all | solution.py:194
  159.7 6.3 %collective-permute-start.16 = (bf16[4,64,256]{2,1,0:T(8,128)(2,1)S(1)}, bf16[4,64,256]{2,1,0:T(8,128)(2,1)S(1)}, u32[]{:S(2)}, u32[]{:S(2)}) collective-permute-start(bf16[4,64,256]{2,1,0:T(8,128)(2,1)S(1)} %reshape.146), channel_id=1, source_target_pairs={{0,1},{1,0},{2,3},{3,2},{4,5},{5,4},{6,7},{7,6},{8,9},{9,8},{10,11... | collective-permute-start | bytes 393224 | tf_op jit(solution)/shard_map/ppermute | solution.py:185
  166.1 14.9 %collective-permute-start.26 = (f32[4,64]{1,0:T(4,128)S(1)}, f32[4,64]{1,0:T(4,128)S(1)}, u32[]{:S(2)}, u32[]{:S(2)}) collective-permute-start(f32[4,64]{1,0:T(4,128)S(1)} %multiply_reduce_fusion), channel_id=1, source_target_pairs={{0,6},{2,0},{4,2},{6,4},{8,14},{10,8},{12,10},{14,12},{16,22},{18,... | collective-permute-start | bytes 3080 | tf_op jit(solution)/shard_map/ppermute | solution.py:94
  169.3 13.9 %collective-permute-start.27 = (f32[4,64]{1,0:T(4,128)S(1)}, f32[4,64]{1,0:T(4,128)S(1)}, u32[]{:S(2)}, u32[]{:S(2)}) collective-permute-start(f32[4,64]{1,0:T(4,128)S(1)} %multiply_reduce_fusion), channel_id=1, source_target_pairs={{0,4},{2,6},{4,0},{6,2},{8,12},{10,14},{12,8},{14,10},{16,20},{18,... | collective-permute-start | bytes 3080 | tf_op jit(solution)/shard_map/ppermute | solution.py:94
  170.2 13.0 %collective-permute-start.28 = (f32[4,64]{1,0:T(4,128)S(1)}, f32[4,64]{1,0:T(4,128)S(1)}, u32[]{:S(2)}, u32[]{:S(2)}) collective-permute-start(f32[4,64]{1,0:T(4,128)S(1)} %multiply_reduce_fusion), channel_id=1, source_target_pairs={{0,2},{2,4},{4,6},{6,0},{8,10},{10,12},{12,14},{14,8},{16,18},{18,... | collective-permute-start | bytes 3080 | tf_op jit(solution)/shard_map/ppermute | solution.py:94
  183.8 5.7 %collective-permute-start.29 = (f32[4,64]{1,0:T(4,128)}, f32[4,64]{1,0:T(4,128)}, u32[]{:S(2)}, u32[]{:S(2)}) collective-permute-start(f32[4,64]{1,0:T(4,128)} %add_add_fusion.1), channel_id=1, source_target_pairs={{0,24},{2,26},{4,28},{6,30},{8,0},{10,2},{12,4},{14,6},{16,8},{18,... | collective-permute-start | bytes 3080 | tf_op jit(solution)/shard_map/ppermute | solution.py:94
  185.5 5.4 %collective-permute-start.30 = (f32[4,64]{1,0:T(4,128)}, f32[4,64]{1,0:T(4,128)}, u32[]{:S(2)}, u32[]{:S(2)}) collective-permute-start(f32[4,64]{1,0:T(4,128)} %add_add_fusion.1), channel_id=1, source_target_pairs={{0,16},{2,18},{4,20},{6,22},{8,24},{10,26},{12,28},{14,30},{16,0},... | collective-permute-start | bytes 3080 | tf_op jit(solution)/shard_map/ppermute | solution.py:94
  197.8 42.7 %collective-permute-start.23 = (bf16[192,1536]{1,0:T(8,128)(2,1)S(1)}, bf16[192,1536]{1,0:T(8,128)(2,1)S(1)}, u32[]{:S(2)}, u32[]{:S(2)}) collective-permute-start(bf16[192,1536]{1,0:T(8,128)(2,1)S(1)} %fusion.10), channel_id=1, source_target_pairs={{0,64},{32,96},{64,128},{96,160},{128,192},{160,224},{192,0},{224,... | collective-permute-start | bytes 1769480 | tf_op jit(solution)/shard_map/ppermute | solution.py:221
  199.9 40.6 %collective-permute-start.24 = (bf16[192,1536]{1,0:T(8,128)(2,1)S(1)}, bf16[192,1536]{1,0:T(8,128)(2,1)S(1)}, u32[]{:S(2)}, u32[]{:S(2)}) collective-permute-start(bf16[192,1536]{1,0:T(8,128)(2,1)S(1)} %fusion.9), channel_id=1, source_target_pairs={{0,128},{32,160},{64,192},{96,224},{128,0},{160,32},{192,64},{224,... | collective-permute-start | bytes 1769480 | tf_op jit(solution)/shard_map/ppermute | solution.py:221
  205.7 36.9 %collective-permute-start.25 = (bf16[192,1536]{1,0:T(8,128)(2,1)S(1)}, bf16[192,1536]{1,0:T(8,128)(2,1)S(1)}, u32[]{:S(2)}, u32[]{:S(2)}) collective-permute-start(bf16[192,1536]{1,0:T(8,128)(2,1)S(1)} %fusion.8), channel_id=1, source_target_pairs={{0,192},{32,224},{64,0},{96,32},{128,64},{160,96},{192,128},{224,1... | collective-permute-start | bytes 1769480 | tf_op jit(solution)/shard_map/ppermute | solution.py:221
  248.8 33.6 %all-to-all-start.1 = ((bf16[16,192,256]{2,1,0:T(8,128)(2,1)}), bf16[16,192,256]{2,1,0:T(8,128)(2,1)S(1)}, u32[]{:S(2)}, u32[]{:S(2)}) async-start(bf16[16,192,256]{2,1,0:T(8,128)(2,1)} %bitcast.74), calls=%async_computation.1 | async-start | bytes 3145728 | tf_op jit(solution)/shard_map/all_to_all | solution.py:231
  282.9 12.3 %collective-permute-start.32 = (bf16[4,64,256]{2,1,0:T(8,128)(2,1)S(1)}, bf16[4,64,256]{2,1,0:T(8,128)(2,1)S(1)}, u32[]{:S(2)}, u32[]{:S(2)}) collective-permute-start(bf16[4,64,256]{2,1,0:T(8,128)(2,1)S(1)} %fusion.34), channel_id=1, source_target_pairs={{0,1},{1,0},{2,3},{3,2},{4,5},{5,4},{6,7},{7,6},{8,9},{9,8},{10,11... | collective-permute-start | bytes 393224 | tf_op jit(solution)/shard_map/ppermute | solution.py:235
  (22 other events, 312.3 us)
Sparse Core Ops, SparseCore 0:
  15.9 73.6 all-gather.1

commit v2 on v0

v2 whole, which is shorter than its diff:
```python
import functools

import jax
import jax.numpy as jnp
from jax import lax
from jax.experimental import pallas as pl
from jax.experimental.pallas import tpu as pltpu
from jax.sharding import PartitionSpec as P

D = 4096
HD = 128
ZH, Y, X = 4, 4, 4
CAP = 48
PLACES = ("rep", "fsdp")
OTHER_HALF = [(0, 1), (1, 0)]
norm_eps = 1e-06
bf16 = jnp.bfloat16
f32 = jnp.float32
i32 = jnp.int32
NT = (((1,), (1,)), ((), ()))
VMEM = pl.BlockSpec(memory_space=pltpu.VMEM)
ANY = pl.BlockSpec(memory_space=pl.ANY)
SMEM = pl.BlockSpec(memory_space=pltpu.SMEM)
ROOM = pltpu.CompilerParams(vmem_limit_bytes=48 * 1024 * 1024)


def across_chip():
    return [(r, r ^ 1) for r in range(2 * ZH)]


def along_z(d):
    return [(r, ((r // 2 + d) % ZH) * 2 + r % 2) for r in range(2 * ZH)]


def swap_zy():
    pairs = []
    for z in range(ZH):
        for c in range(2):
            for y in range(Y):
                for x in range(X):
                    goal = ((y * 2 + c) * Y + z) * X + (x ^ (2 * c))
                    pairs.append((((z * 2 + c) * Y + y) * X + x, goal))
    return pairs


def cost(us):
    return pl.CostEstimate(flops=0, bytes_accessed=us * 3600000, transcendentals=0)


def iota(shape, axis):
    return lax.broadcasted_iota(i32, shape, axis)


def attention_kernel(
    lengths, q, keys, values, nk, nv, out, q_wide, q_rows, fresh, o_rows, ck, cv, arrival
):
    steps, seqs, width = q.shape
    cached = ck.shape[1]
    kv_heads = ck.shape[2] // HD
    group = width // (kv_heads * HD)
    rows = group * steps
    scale = HD ** (-0.5)
    copies = [
        [
            pltpu.make_async_copy(whole.at[b], held.at[b], arrival.at[i, b])
            for i, (whole, held) in enumerate(((keys, ck), (values, cv)))
        ]
        for b in range(seqs)
    ]
    for pair in copies:
        for copy in pair:
            copy.start()
    q_wide[...] = q[...].astype(f32)
    fresh[...] = jnp.zeros_like(fresh)
    place = iota((rows, cached), 1)
    fresh_place = iota((rows, HD), 1)
    live_fresh = fresh_place <= iota((rows, HD), 0) % steps
    for b in range(seqs):
        live = place < lengths[b]
        for copy in copies[b]:
            copy.wait()
        for k in range(kv_heads):
            lanes = pl.ds(k * HD, HD)
            for g in range(group):
                q_rows[pl.ds(g * steps, steps), :] = q_wide[
                    :, b, pl.ds((k * group + g) * HD, HD)
                ]
            for j in range(steps):
                fresh[0, pl.ds(j, 1), :] = nk[j, pl.ds(b, 1), lanes].astype(f32)
                fresh[1, pl.ds(j, 1), :] = nv[j, pl.ds(b, 1), lanes].astype(f32)
            rows_q = q_rows[...].astype(bf16)
            old = lax.dot_general(rows_q, ck[b, :, lanes], NT, preferred_element_type=f32) * scale
            new = (
                lax.dot_general(rows_q, fresh[0].astype(bf16), NT, preferred_element_type=f32) * scale
            )
            old = jnp.where(live, old, -jnp.inf)
            new = jnp.where(live_fresh, new, -jnp.inf)
            top = jnp.maximum(
                jnp.max(old, axis=1, keepdims=True), jnp.max(new, axis=1, keepdims=True)
            )
            old = jnp.exp(old - top)
            new = jnp.exp(new - top)
            share = 1.0 / (
                jnp.sum(old, axis=1, keepdims=True) + jnp.sum(new, axis=1, keepdims=True)
            )
            mixed = jnp.dot(
                (old * share).astype(bf16), cv[b, :, lanes], preferred_element_type=f32
            ) + jnp.dot(
                (new * share).astype(bf16), fresh[1].astype(bf16), preferred_element_type=f32
            )
            for g in range(group):
                o_rows[pl.ds(b * steps, steps), pl.ds((k * group + g) * HD, HD)] = mixed[
                    g * steps : (g + 1) * steps, :
                ]
    done = o_rows[...].astype(bf16)
    for f in range(out.shape[0]):
        out[f] = done


def attention(lengths, q, ck, cv, nk, nv, copies):
    steps, seqs, width = q.shape
    rows = steps * seqs
    group = width // ck.shape[2]
    return pl.pallas_call(
        attention_kernel,
        out_shape=jax.ShapeDtypeStruct((copies, rows, width), bf16),
        in_specs=[SMEM, VMEM, ANY, ANY, VMEM, VMEM],
        out_specs=VMEM,
        scratch_shapes=[
            pltpu.VMEM((steps, seqs, width), f32),
            pltpu.VMEM((group * steps, HD), f32),
            pltpu.VMEM((2, HD, HD), f32),
            pltpu.VMEM((rows, width), f32),
            pltpu.VMEM(ck.shape, bf16),
            pltpu.VMEM(cv.shape, bf16),
            pltpu.SemaphoreType.DMA((2, seqs)),
        ],
        compiler_params=ROOM,
        cost_estimate=cost(7),
        name="attention",
    )(lengths, q, ck, cv, nk, nv)


def project_kernel(place, attn, mine, theirs, out):
    rows, width = out.shape
    steps = 4
    depth = mine.shape[1]
    total = jnp.zeros((rows, width), f32)
    for d in range(ZH):
        for same, held in ((True, mine), (False, theirs)):
            z = lax.rem(place[0] + ZH - d, ZH)
            r = 2 * z + (place[1] if same else 1 - place[1])
            columns = pl.ds(pl.multiple_of(r * depth, depth), depth)
            total = total + jnp.dot(attn[:, columns], held[d], preferred_element_type=f32)
    by_step = jnp.swapaxes(total.reshape(rows // steps, steps, width), 0, 1)
    out[...] = by_step.reshape(rows, width).astype(bf16)


def project(place, attn, mine, theirs):
    return pl.pallas_call(
        project_kernel,
        out_shape=jax.ShapeDtypeStruct((attn.shape[0], mine.shape[2]), bf16),
        in_specs=[SMEM] + [VMEM] * 3,
        out_specs=VMEM,
        compiler_params=ROOM,
        cost_estimate=cost(3),
        name="project",
    )(place, attn, mine, theirs)


def dispatch_kernel(ids, scaled, out):
    experts, slots, _ = out.shape
    top, rows = ids.shape
    block = rows // (slots // CAP)
    expert = iota((experts, rows), 0)
    hit = jnp.zeros((experts, rows), jnp.bool_)
    for k in range(top):
        hit = hit | (ids[pl.ds(k, 1), :] == expert)
    before, after = iota((rows, rows), 0), iota((rows, rows), 1)
    earlier = (before <= after) & (before // block == after // block)
    rank = jnp.dot(
        hit.astype(f32).astype(bf16), earlier.astype(f32).astype(bf16), preferred_element_type=f32
    ).astype(i32)
    slot_of = jnp.where(hit, iota((experts, rows), 1) // block * CAP + rank - 1, -1)
    slot = iota((slots, rows), 0)
    for e in range(experts):
        pick = jnp.where(slot_of[e : e + 1, :] == slot, f32(1.0), f32(0.0)).astype(bf16)
        out[e] = jnp.dot(pick, scaled[...], preferred_element_type=f32).astype(bf16)


def dispatch(ids, scaled, experts, steps):
    return pl.pallas_call(
        dispatch_kernel,
        out_shape=jax.ShapeDtypeStruct((experts, steps * CAP, scaled.shape[1]), bf16),
        in_specs=[VMEM] * 2,
        out_specs=VMEM,
        compiler_params=ROOM,
        cost_estimate=cost(2),
        name="dispatch",
    )(ids, scaled)


def expand_rows(place, arrived, near, far, ahead):
    total = None
    for i in range(4):
        held = (near, far)[i // 2][i % 2]
        rows = jnp.concatenate([arrived[4 * lax.rem(place[0] + d, ZH) + i] for d in ahead])
        part = jnp.dot(rows, held, preferred_element_type=f32)
        total = part if total is None else total + part
    return total


def expand_far_kernel(place, arrived, near, far, low, high):
    total = expand_rows(place, arrived, near, far, (2,))
    half = total.shape[0] // 2
    low[...] = total[:half].astype(bf16)
    high[...] = total[half:].astype(bf16)


def expand_near_kernel(place, arrived, near, far, plus, minus, own):
    total = expand_rows(place, arrived, near, far, (1, 3, 0))
    slots = own.shape[0]
    for i, out in enumerate((plus, minus, own)):
        out[...] = total[i * slots : (i + 1) * slots]


def expand_far(place, arrived, near, far):
    half, width = arrived.shape[1] // 2, near.shape[2]
    return pl.pallas_call(
        expand_far_kernel,
        out_shape=[jax.ShapeDtypeStruct((half, width), bf16)] * 2,
        in_specs=[SMEM] + [VMEM] * 3,
        out_specs=[VMEM] * 2,
        compiler_params=ROOM,
        cost_estimate=cost(2),
        name="expand_far",
    )(place, arrived, near, far)


def expand_near(place, arrived, near, far):
    slots, width = arrived.shape[1], near.shape[2]
    return pl.pallas_call(
        expand_near_kernel,
        out_shape=[jax.ShapeDtypeStruct((slots, width), f32)] * 3,
        in_specs=[SMEM] + [VMEM] * 3,
        out_specs=[VMEM] * 3,
        compiler_params=ROOM,
        cost_estimate=cost(4),
        name="expand_near",
    )(place, arrived, near, far)


def contract_kernel(steps, place, ids, squares, own, one, two, *refs):
    *weights, out = refs
    slots, width = out.shape[1:]
    half = own.shape[1] // 2
    top, rows = ids.shape
    block = rows // steps
    total = jnp.sum(squares[...], axis=0, keepdims=True)
    row_scale = lax.rsqrt(total / D + norm_eps)
    hit = jnp.zeros((8, rows), jnp.bool_)
    for k in range(top):
        hit = hit | (jnp.broadcast_to(ids[pl.ds(k, 1), :], (8, rows)) == place[2])
    before, after = iota((rows, rows), 0), iota((rows, rows), 1)
    earlier = (before <= after) & (before // block == after // block)
    rank = jnp.dot(
        hit.astype(f32).astype(bf16), earlier.astype(f32).astype(bf16), preferred_element_type=f32
    ).astype(i32)
    slot_of = jnp.where(hit, iota((8, rows), 1) // block * CAP + rank - 1, -1)
    pick = slot_of[0:1, :] == iota((slots, rows), 0)
    slot_scale = jnp.sum(jnp.where(pick, row_scale, 0.0), axis=1, keepdims=True)
    both = (own[...] + (one[...].astype(f32) + two[...].astype(f32))) * slot_scale
    gate, up = both[:, :half], both[:, half:]
    hidden = (gate / (1.0 + jnp.exp(-gate)) * up).astype(bf16)
    split = half // 2
    for r in range(weights[0].shape[0]):
        result = jnp.dot(hidden[:, :split], weights[0][r], preferred_element_type=f32)
        result = result + jnp.dot(hidden[:, split:], weights[1][r], preferred_element_type=f32)
        for i in range(2):
            out[2 * r + i] = result[:, i * width : (i + 1) * width].astype(bf16)


def contract(steps, place, ids, squares, parts, weights, experts, width):
    slots = parts[0].shape[0]
    return pl.pallas_call(
        functools.partial(contract_kernel, steps),
        out_shape=jax.ShapeDtypeStruct((experts, slots, width), bf16),
        in_specs=[SMEM] + [VMEM] * (2 + len(parts) + len(weights)),
        out_specs=VMEM,
        compiler_params=ROOM,
        cost_estimate=cost(5),
        name="contract",
    )(place, ids, squares, *parts, *weights)


def combine_kernel(steps, ids, gates, *refs):
    *returned, out = refs
    experts, slots, _ = returned[0].shape
    rows, top = ids.shape
    block = rows // steps
    expert = iota((rows, experts), 1)
    hit = jnp.zeros((rows, experts), jnp.bool_)
    gate = jnp.zeros((rows, experts), f32)
    wide_gates = gates[...].astype(f32)
    for k in range(top):
        named = ids[:, k : k + 1] == expert
        hit = hit | named
        gate = jnp.where(named, wide_gates[:, k : k + 1], gate)
    after, before = iota((rows, rows), 0), iota((rows, rows), 1)
    earlier = (before <= after) & (before // block == after // block)
    rank = jnp.dot(
        earlier.astype(f32).astype(bf16), hit.astype(f32).astype(bf16), preferred_element_type=f32
    ).astype(i32)
    slot_of = jnp.where(hit, iota((rows, experts), 0) // block * CAP + rank - 1, -1)
    part = rows // len(returned)
    for i, held in enumerate(returned):
        slot = iota((part, slots), 1) + i * slots
        total = jnp.zeros((part, out.shape[1]), f32)
        of, by = slot_of[i * part : (i + 1) * part], gate[i * part : (i + 1) * part]
        for e in range(experts):
            weights = jnp.where(of[:, e : e + 1] == slot, by[:, e : e + 1], 0.0).astype(bf16)
            total = total + jnp.dot(weights, held[e], preferred_element_type=f32)
        out[pl.ds(i * part, part), :] = total.astype(bf16)


def combine(steps, ids, gates, returned):
    return pl.pallas_call(
        functools.partial(combine_kernel, steps),
        out_shape=jax.ShapeDtypeStruct((ids.shape[0], returned[0].shape[2]), bf16),
        in_specs=[VMEM] * (2 + len(returned)),
        out_specs=VMEM,
        compiler_params=ROOM,
        cost_estimate=cost(2),
        name="combine",
    )(ids, gates, *returned)


def on_device(
    queries,
    cache_keys,
    cache_values,
    new_keys,
    new_values,
    lengths,
    attn_out_weight,
    residual,
    norm_gain,
    expert_ids,
    gate_weights,
    expert_in,
    expert_out,
):
    rep, fsdp = lax.axis_index("rep"), lax.axis_index("fsdp")
    z, c = rep // 2, rep % 2
    place = jnp.stack([z, c, fsdp, lax.axis_index("tp")]).astype(i32)
    steps, block, top = expert_ids.shape
    experts = Y * X
    rows, model = steps * block, residual.shape[2]
    ids_by_step = expert_ids.reshape(rows, top)
    ids_across = jnp.transpose(ids_by_step)

    def shift(value, d):
        return lax.ppermute(value, "rep", along_z(d))

    def core(value):
        return lax.ppermute(value, "rep", across_chip())

    proj_minus, proj_plus = shift(attn_out_weight, 1), shift(attn_out_weight, -1)
    ids_there = lax.ppermute(ids_across, PLACES, swap_zy())
    attn = attention(lengths, queries, cache_keys, cache_values, new_keys, new_values, experts)
    quarter = expert_out.shape[1] // 2
    out_first, out_second = expert_out[0, :quarter], expert_out[0, quarter:]
    attn, ids_there, proj_minus, proj_plus, out_first = lax.optimization_barrier(
        (attn, ids_there, proj_minus, proj_plus, out_first)
    )
    out_first = lax.all_gather(out_first, "rep", axis=0, tiled=False)
    split = proj_minus.shape[0] // 2
    proj_far = [shift(proj_minus[:split], 1), shift(proj_plus[split:], -1)]

    near_in = expert_in[0].reshape(expert_in.shape[1], -1)
    attn, near_in = lax.optimization_barrier((attn, near_in))
    far_in = core(near_in)
    attn = lax.all_to_all(attn, "fsdp", split_axis=0, concat_axis=0, tiled=True)
    mine = jnp.stack([attn_out_weight, proj_minus, jnp.concatenate(proj_far), proj_plus])
    attn, mine, theirs = lax.optimization_barrier((attn, mine, core(mine)))
    near_in, far_in = near_in.reshape(2, model, -1), far_in.reshape(2, model, -1)
    partial = project(place, attn.reshape(rows, -1), mine, theirs)
    here_cross = lax.ppermute(partial, "tp", OTHER_HALF)
    attended = residual.astype(f32).reshape(rows, model) + (
        partial.astype(f32) + here_cross.astype(f32)
    )
    scaled = (attended * norm_gain).astype(bf16)
    there = lax.ppermute(scaled, PLACES, swap_zy())

    there, out_second = lax.optimization_barrier((there, out_second))
    out_second = lax.all_gather(out_second, "rep", axis=0, tiled=False)
    dispatched = dispatch(ids_there, there, experts, steps)
    arrived = lax.all_to_all(dispatched, "fsdp", split_axis=0, concat_axis=0, tiled=True)

    low, high = expand_far(place, arrived, near_in, far_in)
    low, high = shift(low, 1), shift(high, -1)
    plus, minus, own = expand_near(place, arrived, near_in, far_in)
    half = low.shape[0]
    low, high, plus, minus = lax.optimization_barrier((low, high, plus, minus))
    plus = jnp.concatenate([plus[:half] + low.astype(f32), plus[half:]]).astype(bf16)
    minus = jnp.concatenate([minus[:half], minus[half:] + high.astype(f32)]).astype(bf16)
    squares = jnp.sum(attended * attended, axis=-1).reshape(steps, block)
    squares, plus, minus = lax.optimization_barrier((squares, plus, minus))
    plus, minus = shift(plus, 1), shift(minus, -1)
    squares = lax.all_gather(squares, "fsdp", axis=0, tiled=False).reshape(experts, rows)

    result = contract(
        steps,
        place,
        ids_across,
        squares,
        [own, plus, minus],
        [out_first, out_second],
        experts,
        model,
    )
    returned = lax.all_to_all(result, "fsdp", split_axis=0, concat_axis=0, tiled=True)
    routed = combine(steps, ids_by_step, gate_weights.reshape(rows, top), [returned])
    routed_cross = lax.ppermute(routed, "tp", OTHER_HALF)
    routed = routed.astype(f32) + routed_cross.astype(f32)
    return (attended + routed).astype(bf16).reshape(steps, block, model)


def solution(mesh):
    placed = (
        P(None, ("rep", "fsdp"), "tp"),
        P(("rep", "fsdp"), None, "tp"),
        P(("rep", "fsdp"), None, "tp"),
        P(None, ("rep", "fsdp"), "tp"),
        P(None, ("rep", "fsdp"), "tp"),
        P(("rep", "fsdp")),
        P(("tp", "rep"), "fsdp"),
        P(None, "rep", "fsdp"),
        P("fsdp"),
        P(None, "rep", None),
        P(None, "rep", None),
        P("fsdp", "rep", None, "tp"),
        P("fsdp", "tp", "rep"),
    )
    return jax.shard_map(
        on_device, mesh=mesh, in_specs=placed, out_specs=P(None, "rep", "fsdp"), check_vma=False
    )
```

time: 465 us -> 238 us (0.51)
  waiting for transfers between devices: 258 us -> 79.8 us
  blocking collectives: 135 us -> 27.5 us
  starting transfers between devices: 7.28 us -> 76.4 us
  Pallas kernels: 0 us -> 24.8 us
  local copies, waits for them, and re-layouts: 29.9 us -> 10.3 us
  matrix products: 18.6 us -> 0 us
    all_gather x4 -> x2, waiting for transfers between devices: 201 us -> 0.03 us  [the longest x1 0.02 us: on_device(): out_second = lax.all_gather(out_second, 'rep', axis=0, tiled=False)]
    psum x2 -> x0, blocking collectives: 117 us -> none  [the longest x1 77 us: on_device(): lax.psum(expert_result.reshape(1, step_count, capacity, experts, column_w...]
    ppermute x0 -> x14, starting transfers between devices: none -> 36.5 us  [the longest x8 16.9 us: shift(): return lax.ppermute(value, 'rep', along_z(d))]
    all_to_all x1 -> x3, waiting for transfers between devices: 23.1 us -> 59.1 us  [the longest x1 24.8 us: on_device(): lax.all_to_all(dispatched, 'fsdp', split_axis=0, concat_axis=0, tiled=True)]
    all_to_all x1 -> x3, starting transfers between devices: 7.11 us -> 39.8 us  [the longest x1 17 us: on_device(): lax.all_to_all(dispatched, 'fsdp', split_axis=0, concat_axis=0, tiled=True)]
    psum x1 -> x0, waiting for transfers between devices: 31.7 us -> none  [on_device(): projected = lax.psum(partial_proj, 'tp')]
    all_gather x0 -> x1, blocking collectives: none -> 27.5 us  [on_device(): lax.all_gather(squares, 'fsdp', axis=0, tiled=False).reshape(experts, rows)]
    pallas_call x0 -> x7, Pallas kernels: none -> 24.8 us  [the longest x1 6.3 us: contract(): pl.pallas_call(functools.partial(contract_kernel, steps), out_shape=jax.S...]
  transfers between devices with their start and end apart: 6 -> 19, of which waited for: 6 -> 10; matrix products, arithmetic and copies ran while one was open for 6% -> 3% of each run, Pallas kernels for 0% -> 7%
where the time goes in v2:
time: 238 us; the launch traced here: 237 us
  waiting for transfers between devices  79.8 us (34%)
  starting transfers between devices  76.4 us (32%)
  blocking collectives  27.5 us (12%)
  Pallas kernels  24.8 us (10%)
  between operations  13.7 us (6%)
  local copies, waits for them, and re-layouts  10.3 us (4%)
  other arithmetic  4.24 us (2%)
    all_gather x1, blocking collectives, on_device(): lax.all_gather(squares, 'fsdp', axis=0, tiled=False).reshape(experts, rows)  27.5 us
    all_to_all x1, waiting for transfers between devices, on_device(): lax.all_to_all(dispatched, 'fsdp', split_axis=0, concat_axis=0, tiled=True)  24.8 us
    all_to_all x1, waiting for transfers between devices, on_device(): lax.all_to_all(result, 'fsdp', split_axis=0, concat_axis=0, tiled=True)  17.2 us
    all_to_all x1, waiting for transfers between devices, on_device(): attn = lax.all_to_all(attn, 'fsdp', split_axis=0, concat_axis=0, tiled=True)  17.2 us
    all_to_all x1, starting transfers between devices, on_device(): lax.all_to_all(dispatched, 'fsdp', split_axis=0, concat_axis=0, tiled=True)  17 us
    ppermute x8, starting transfers between devices, shift(): return lax.ppermute(value, 'rep', along_z(d))  16.9 us
    all_to_all x1, starting transfers between devices, on_device(): attn = lax.all_to_all(attn, 'fsdp', split_axis=0, concat_axis=0, tiled=True)  14.6 us
    ppermute x1, starting transfers between devices, on_device(): routed_cross = lax.ppermute(routed, 'tp', OTHER_HALF)  9.89 us
  transfers between devices with their start and end apart: 19, of which 10 were waited for; matrix products, arithmetic and copies ran while one was open for 3% of the time, Pallas kernels for 7%

profile of v2, /device:TPU:32, one launch (start us, length us, event | category | flops | bytes accessed | tf_op | source)
XLA Modules:
  0.0 236.6 jit_solution(4117761867200911927)
XLA Ops:
  6.6 3.3 %collective-permute-start.1 = (bf16[512,256]{1,0:T(8,128)(2,1)}, bf16[512,256]{1,0:T(8,128)(2,1)S(1)}, u32[]{:S(2)}, u32[]{:S(2)}) collective-permute-start(bf16[512,256]{1,0:T(8,128)(2,1)} %param.19), channel_id=1, source_target_pairs={{0,64},{32,96},{64,128},{96,160},{128,192},{160,224},{192,0},{224,... | collective-permute-start | bytes 786440 | tf_op jit(solution)/shard_map/ppermute | solution.py:363
  9.9 2.2 collective-permute-start.2
  13.6 2.1 slice_bitcast_fusion
  15.8 1.6 copy-done.3
  17.3 6.2 %attention.1 = bf16[16,16,4096]{2,1,0:T(8,128)(2,1)S(1)} custom-call(s32[4]{0:T(128)S(1)} %copy-done.7, bf16[4,4,4096]{2,1,0:T(4,128)(2,1)S(1)} %copy-done.4, bf16[4,1024,256]{2,1,0:T(8,128)(2,1)S(1)} %copy-done.3, bf16[4,1024,256]{2,1,0:T(8,128)(2,1)} %values.1, bf16[4,4,256]{2,1,0:T(4,128)(2,1)S(1)} %copy-done.5, bf16[4,4,256]{2,1,0:T(4,128)(2,1)S(1)} %copy-done.6), custom_call_target="tpu_custom_call" | custom-call | bytes 25200000 | tf_op jit(solution)/shard_map/attention/pallas_call | solution.py:124
  23.6 1.3 copy-done.1
  26.0 14.6 %all-to-all-start = ((bf16[16,16,4096]{2,1,0:T(8,128)(2,1)}), bf16[16,16,4096]{2,1,0:T(8,128)(2,1)}, u32[]{:S(2)}, u32[]{:S(2)}) async-start(bf16[16,16,4096]{2,1,0:T(8,128)(2,1)} %copy-done.1), calls=%async_computation | async-start | bytes 4194304 | tf_op jit(solution)/shard_map/all_to_all | solution.py:383
  40.6 2.4 %collective-permute-start.3 = (bf16[256,256]{1,0:T(8,128)(2,1)S(1)}, bf16[256,256]{1,0:T(8,128)(2,1)S(1)}, u32[]{:S(2)}, u32[]{:S(2)}) collective-permute-start(bf16[256,256]{1,0:T(8,128)(2,1)S(1)} %slice.27), channel_id=1, source_target_pairs={{0,64},{32,96},{64,128},{96,160},{128,192},{160,224},{192,0},{224,... | collective-permute-start | bytes 393224 | tf_op jit(solution)/shard_map/ppermute | solution.py:363
  43.9 1.9 collective-permute-start.4
  45.8 2.3 collective-permute-done.3
  48.2 2.6 %collective-permute-done.4 = bf16[256,256]{1,0:T(8,128)(2,1)S(1)} collective-permute-done((bf16[256,256]{1,0:T(8,128)(2,1)S(1)}, bf16[256,256]{1,0:T(8,128)(2,1)S(1)}, u32[]{:S(2)}, u32[]{:S(2)}) %collective-permute-start.4) | collective-permute-done | bytes 131104 | tf_op jit(solution)/shard_map/ppermute | solution.py:363
  52.1 2.7 %collective-permute-done.5.theirs = bf16[4,512,256]{2,1,0:T(8,128)(2,1)} collective-permute-done((bf16[4,512,256]{2,1,0:T(8,128)(2,1)S(1)}, bf16[4,512,256]{2,1,0:T(8,128)(2,1)}, u32[]{:S(2)}, u32[]{:S(2)}) %collective-permute-start.5) | collective-permute-done | bytes 1048608 | tf_op jit(solution)/shard_map/ppermute | solution.py:366
  54.8 17.2 %all-to-all-done = bf16[16,16,4096]{2,1,0:T(8,128)(2,1)} async-done(((bf16[16,16,4096]{2,1,0:T(8,128)(2,1)}), bf16[16,16,4096]{2,1,0:T(8,128)(2,1)}, u32[]{:S(2)}, u32[]{:S(2)}) %all-to-all-start) | async-done | bytes 2097184 | tf_op jit(solution)/shard_map/all_to_all | solution.py:383
  72.0 2.7 %project.1 = bf16[256,256]{1,0:T(8,128)(2,1)S(1)} custom-call(s32[4]{0:T(128)S(1)} %pad_add_fusion.place, bf16[256,4096]{1,0:T(8,128)(2,1)} %bitcast.12.attn, bf16[4,512,256]{2,1,0:T(8,128)(2,1)S(1)} %pad_maximum_fusion.mine, bf16[4,512,256]{2,1,0:T(8,128)(2,1)} %collective-permute-done.5.theirs), custom_call_target="tpu_custom_call" | custom-call | bytes 10800000 | tf_op jit(solution)/shard_map/project/pallas_call | solution.py:160
  74.6 1.7 collective-permute-start.6
  76.3 5.3 %collective-permute-done.6 = bf16[256,256]{1,0:T(8,128)(2,1)S(1)} collective-permute-done((bf16[256,256]{1,0:T(8,128)(2,1)S(1)}, bf16[256,256]{1,0:T(8,128)(2,1)S(1)}, u32[]{:S(2)}, u32[]{:S(2)}) %collective-permute-start.6) | collective-permute-done | bytes 131104 | tf_op jit(solution)/shard_map/ppermute | solution.py:388
  82.9 6.6 %collective-permute-start.8 = (bf16[512,1536]{1,0:T(8,128)(2,1)S(1)}, bf16[512,1536]{1,0:T(8,128)(2,1)}, u32[]{:S(2)}, u32[]{:S(2)}) collective-permute-start(bf16[512,1536]{1,0:T(8,128)(2,1)S(1)} %bitcast.36), channel_id=1, source_target_pairs={{0,32},{32,0},{64,96},{96,64},{128,160},{160,128},{192,224},{224,1... | collective-permute-start | bytes 4718600 | tf_op jit(solution)/shard_map/ppermute | solution.py:366
  91.5 17.0 %all-to-all-start.1 = ((bf16[16,192,256]{2,1,0:T(8,128)(2,1)}), bf16[16,192,256]{2,1,0:T(8,128)(2,1)S(1)}, u32[]{:S(2)}, u32[]{:S(2)}) async-start(bf16[16,192,256]{2,1,0:T(8,128)(2,1)} %copy-done.2), calls=%async_computation.1 | async-start | bytes 3145728 | tf_op jit(solution)/shard_map/all_to_all | solution.py:398
  108.5 24.8 %all-to-all-done.1.arrived = bf16[16,192,256]{2,1,0:T(8,128)(2,1)S(1)} async-done(((bf16[16,192,256]{2,1,0:T(8,128)(2,1)}), bf16[16,192,256]{2,1,0:T(8,128)(2,1)S(1)}, u32[]{:S(2)}, u32[]{:S(2)}) %all-to-all-start.1) | async-done | bytes 1572896 | tf_op jit(solution)/shard_map/all_to_all | solution.py:398
  133.2 3.0 %expand_far.1 = (bf16[96,1536]{1,0:T(8,128)(2,1)}, bf16[96,1536]{1,0:T(8,128)(2,1)}) custom-call(s32[4]{0:T(128)S(1)} %pad_add_fusion.place, bf16[16,192,256]{2,1,0:T(8,128)(2,1)S(1)} %all-to-all-done.1.arrived, bf16[2,256,1536]{2,1,0:T(8,128)(2,1)S(1)} %bitcast.37, bf16[2,256,1536]{2,1,0:T(8,128)(2,1)} %bitcast.17.far), custom_call_target="tpu_custom_call" | custom-call | bytes 7200000 | tf_op jit(solution)/shard_map/expand_far/pallas_call | solution.py:229
  137.4 1.8 collective-permute-start.9
  139.2 3.9 %expand_near.1 = (f32[192,1536]{1,0:T(8,128)S(1)}, f32[192,1536]{1,0:T(8,128)S(1)}, f32[192,1536]{1,0:T(8,128)S(1)}) custom-call(s32[4]{0:T(128)S(1)} %pad_add_fusion.place, bf16[16,192,256]{2,1,0:T(8,128)(2,1)S(1)} %all-to-all-done.1.arrived, bf16[2,256,1536]{2,1,0:T(8,128)(2,1)} %bitcast.38, bf16[2,256,1536]{2,1,0:T(8,128)(2,1)} %bitcast.17.far), custom_call_target="tpu_custom_call" | custom-call | bytes 14400000 | tf_op jit(solution)/shard_map/expand_near/pallas_call | solution.py:242
  143.1 4.5 %collective-permute-done.10 = bf16[96,1536]{1,0:T(8,128)(2,1)S(1)} collective-permute-done((bf16[96,1536]{1,0:T(8,128)(2,1)}, bf16[96,1536]{1,0:T(8,128)(2,1)S(1)}, u32[]{:S(2)}, u32[]{:S(2)}) %collective-permute-start.10) | collective-permute-done | bytes 294944 | tf_op jit(solution)/shard_map/ppermute | solution.py:363
  150.5 1.5 collective-permute-start.11
  151.9 2.7 %collective-permute-start.12 = (bf16[192,1536]{1,0:T(8,128)(2,1)S(1)}, bf16[192,1536]{1,0:T(8,128)(2,1)S(1)}, u32[]{:S(2)}, u32[]{:S(2)}) collective-permute-start(bf16[192,1536]{1,0:T(8,128)(2,1)S(1)} %pad_maximum_fusion.2), channel_id=1, source_target_pairs={{0,192},{32,224},{64,0},{96,32},{128,64},{160,96},{192,128},{224,1... | collective-permute-start | bytes 1769480 | tf_op jit(solution)/shard_map/ppermute | solution.py:363
  154.7 27.5 %all-gather.3 = f32[16,4,64]{2,1,0:T(4,128)S(1)} all-gather(f32[1,4,64]{2,1,0:T(4,128)S(1)} %bitcast.48), channel_id=2, replica_groups=mesh['rep'=8,'fsdp'=16,'tp'=2] {'fsdp'}, dimensions={0}, use_global_device_ids=true | all-gather | bytes 17408 | tf_op jit(solution)/shard_map/all_gather | solution.py:410
  182.3 6.3 %contract.1 = bf16[16,192,256]{2,1,0:T(8,128)(2,1)} custom-call(s32[4]{0:T(128)S(1)} %pad_add_fusion.place, s32[8,256]{1,0:T(8,128)S(1)} %copy.21.ids, f32[16,256]{1,0:T(8,128)S(1)} %reshape.39.squares, f32[192,1536]{1,0:T(8,128)S(1)} %get-tuple-element.48.own, bf16[192,1536]{1,0:T(8,128)(2,1)S(1)} %collective-permute-done.11.one, ...), custom_call_target="tpu_custom_call" | custom-call | bytes 18000000 | tf_op jit(solution)/shard_map/contract/pallas_call | solution.py:285
  188.6 8.3 %all-to-all-start.2 = ((bf16[16,192,256]{2,1,0:T(8,128)(2,1)}), bf16[16,192,256]{2,1,0:T(8,128)(2,1)S(1)}, u32[]{:S(2)}, u32[]{:S(2)}) async-start(bf16[16,192,256]{2,1,0:T(8,128)(2,1)} %contract.1), calls=%async_computation.2 | async-start | bytes 3145728 | tf_op jit(solution)/shard_map/all_to_all | solution.py:422
  197.0 17.2 %all-to-all-done.2.refs_0_ = bf16[16,192,256]{2,1,0:T(8,128)(2,1)S(1)} async-done(((bf16[16,192,256]{2,1,0:T(8,128)(2,1)}), bf16[16,192,256]{2,1,0:T(8,128)(2,1)S(1)}, u32[]{:S(2)}, u32[]{:S(2)}) %all-to-all-start.2) | async-done | bytes 1572896 | tf_op jit(solution)/shard_map/all_to_all | solution.py:422
  214.2 2.0 combine.1
  216.2 9.9 %collective-permute-start.13 = (bf16[256,256]{1,0:T(8,128)(2,1)S(1)}, bf16[256,256]{1,0:T(8,128)(2,1)S(1)}, u32[]{:S(2)}, u32[]{:S(2)}) collective-permute-start(bf16[256,256]{1,0:T(8,128)(2,1)S(1)} %combine.1), channel_id=1, source_target_pairs={{0,1},{1,0},{2,3},{3,2},{4,5},{5,4},{6,7},{7,6},{8,9},{9,8},{10,11... | collective-permute-start | bytes 393224 | tf_op jit(solution)/shard_map/ppermute | solution.py:424
  226.1 2.9 %collective-permute-done.13 = bf16[256,256]{1,0:T(8,128)(2,1)S(1)} collective-permute-done((bf16[256,256]{1,0:T(8,128)(2,1)S(1)}, bf16[256,256]{1,0:T(8,128)(2,1)S(1)}, u32[]{:S(2)}, u32[]{:S(2)}) %collective-permute-start.13) | collective-permute-done | bytes 131104 | tf_op jit(solution)/shard_map/ppermute | solution.py:424
  (74 shorter events, 13.2 us)
Async XLA Ops:
  6.5 9.2 %copy-start.4 = (bf16[4,4,4096]{2,1,0:T(4,128)(2,1)S(1)}, bf16[4,4,4096]{2,1,0:T(4,128)(2,1)}, u32[]{:S(2)}) copy-start(bf16[4,4,4096]{2,1,0:T(4,128)(2,1)} %q.1) | copy-start | bytes 393220
  6.5 9.2 %copy-start.5 = (bf16[4,4,256]{2,1,0:T(4,128)(2,1)S(1)}, bf16[4,4,256]{2,1,0:T(4,128)(2,1)}, u32[]{:S(2)}) copy-start(bf16[4,4,256]{2,1,0:T(4,128)(2,1)} %nk.1) | copy-start | bytes 24580
  6.5 9.2 %copy-start.6 = (bf16[4,4,256]{2,1,0:T(4,128)(2,1)S(1)}, bf16[4,4,256]{2,1,0:T(4,128)(2,1)}, u32[]{:S(2)}) copy-start(bf16[4,4,256]{2,1,0:T(4,128)(2,1)} %nv.1) | copy-start | bytes 24580
  6.5 9.2 %copy-start.7 = (s32[4]{0:T(128)S(1)}, s32[4]{0:T(128)}, u32[]{:S(2)}) copy-start(s32[4]{0:T(128)} %lengths.1) | copy-start | bytes 52
  6.5 175.7 %all-gather.7.cloned.1.call-start = ((), (), s32[]{:S(2)}) async-start(), calls=%async_computation.3 | async-start | bytes 3538944 | tf_op jit(solution)/shard_map/all_gather | solution.py:376
  6.6 18.3 %collective-permute-start.1 = (bf16[512,256]{1,0:T(8,128)(2,1)}, bf16[512,256]{1,0:T(8,128)(2,1)S(1)}, u32[]{:S(2)}, u32[]{:S(2)}) collective-permute-start(bf16[512,256]{1,0:T(8,128)(2,1)} %param.19), channel_id=1, source_target_pairs={{0,64},{32,96},{64,128},{96,160},{128,192},{160,224},{192,0},{224,... | collective-permute-start | bytes 786440 | tf_op jit(solution)/shard_map/ppermute | solution.py:363
  9.9 15.0 %collective-permute-start.2 = (bf16[512,256]{1,0:T(8,128)(2,1)}, bf16[512,256]{1,0:T(8,128)(2,1)}, u32[]{:S(2)}, u32[]{:S(2)}) collective-permute-start(bf16[512,256]{1,0:T(8,128)(2,1)} %param.19), channel_id=1, source_target_pairs={{0,192},{32,224},{64,0},{96,32},{128,64},{160,96},{192,128},{224,1... | collective-permute-start | bytes 786440 | tf_op jit(solution)/shard_map/ppermute | solution.py:363
  13.0 11.9 %collective-permute-start = (s32[8,256]{0,1:T(8,128)S(1)}, s32[8,256]{0,1:T(8,128)S(1)}, u32[]{:S(2)}, u32[]{:S(2)}) collective-permute-start(s32[8,256]{0,1:T(8,128)S(1)} %bitcast.39), channel_id=1, source_target_pairs={{0,0},{2,2},{4,4},{6,6},{8,64},{10,66},{12,68},{14,70},{16,128},{1... | collective-permute-start | bytes 24584 | tf_op jit(solution)/shard_map/ppermute | solution.py:369
  15.7 1.6 copy-start.3
  17.3 8.3 %copy-start.8 = (bf16[1,512,2,768]{3,2,1,0:T(2,128)(2,1)S(1)}, bf16[1,512,2,768]{3,2,1,0:T(2,128)(2,1)}, u32[]{:S(2)}) copy-start(bf16[1,512,2,768]{3,2,1,0:T(2,128)(2,1)} %param.24) | copy-start | bytes 4718596
  26.0 107.3 %copy-start = (bf16[64,8,2,768]{3,1,2,0:T(8,128)(2,1)}, bf16[64,8,2,768]{3,1,2,0:T(8,128)(2,1)S(1)}, u32[]{:S(2)}) copy-start(bf16[64,8,2,768]{3,1,2,0:T(8,128)(2,1)S(1)} %copy.22) | copy-start | bytes 4718596
  26.0 14.6 %copy-start.10 = (bf16[512,256]{1,0:T(8,128)(2,1)S(1)}, bf16[512,256]{1,0:T(8,128)(2,1)}, u32[]{:S(2)}) copy-start(bf16[512,256]{1,0:T(8,128)(2,1)} %copy-done.9) | copy-start | bytes 786436
  26.0 46.0 %all-to-all-start = ((bf16[16,16,4096]{2,1,0:T(8,128)(2,1)}), bf16[16,16,4096]{2,1,0:T(8,128)(2,1)}, u32[]{:S(2)}, u32[]{:S(2)}) async-start(bf16[16,16,4096]{2,1,0:T(8,128)(2,1)} %copy-done.1), calls=%async_computation | async-start | bytes 4194304 | tf_op jit(solution)/shard_map/all_to_all | solution.py:383
  40.6 141.7 %all-gather.9.cloned.1.call-start = ((), (), s32[]{:S(2)}) async-start(), calls=%async_computation.4 | async-start | bytes 3538944 | tf_op jit(solution)/shard_map/all_gather | solution.py:396
  40.6 7.5 %collective-permute-start.3 = (bf16[256,256]{1,0:T(8,128)(2,1)S(1)}, bf16[256,256]{1,0:T(8,128)(2,1)S(1)}, u32[]{:S(2)}, u32[]{:S(2)}) collective-permute-start(bf16[256,256]{1,0:T(8,128)(2,1)S(1)} %slice.27), channel_id=1, source_target_pairs={{0,64},{32,96},{64,128},{96,160},{128,192},{160,224},{192,0},{224,... | collective-permute-start | bytes 393224 | tf_op jit(solution)/shard_map/ppermute | solution.py:363
  43.9 6.8 %collective-permute-start.4 = (bf16[256,256]{1,0:T(8,128)(2,1)S(1)}, bf16[256,256]{1,0:T(8,128)(2,1)S(1)}, u32[]{:S(2)}, u32[]{:S(2)}) collective-permute-start(bf16[256,256]{1,0:T(8,128)(2,1)S(1)} %slice.28), channel_id=1, source_target_pairs={{0,192},{32,224},{64,0},{96,32},{128,64},{160,96},{192,128},{224,1... | collective-permute-start | bytes 393224 | tf_op jit(solution)/shard_map/ppermute | solution.py:363
  51.9 2.9 %collective-permute-start.5 = (bf16[4,512,256]{2,1,0:T(8,128)(2,1)S(1)}, bf16[4,512,256]{2,1,0:T(8,128)(2,1)}, u32[]{:S(2)}, u32[]{:S(2)}) collective-permute-start(bf16[4,512,256]{2,1,0:T(8,128)(2,1)S(1)} %pad_maximum_fusion.mine), channel_id=1, source_target_pairs={{0,32},{32,0},{64,96},{96,64},{128,160},{160,128},{192,224},{224,1... | collective-permute-start | bytes 3145736 | tf_op jit(solution)/shard_map/ppermute | solution.py:366
  72.0 9.6 %copy-start.11 = (bf16[4,64,256]{2,1,0:T(8,128)(2,1)S(1)}, bf16[4,64,256]{2,1,0:T(8,128)(2,1)}, u32[]{:S(2)}) copy-start(bf16[4,64,256]{2,1,0:T(8,128)(2,1)} %param.20) | copy-start | bytes 393220
  72.0 9.6 %copy-start.18 = (f32[256]{0:T(256)S(1)}, f32[256]{0:T(256)}, u32[]{:S(2)}) copy-start(f32[256]{0:T(256)} %param.21) | copy-start | bytes 3076
  72.0 17.5 %copy-start.16 = (s32[8,256]{0,1:T(8,128)S(1)}, s32[8,256]{0,1:T(8,128)}, u32[]{:S(2)}) copy-start(s32[8,256]{0,1:T(8,128)} %copy-done.15) | copy-start | bytes 24580
  74.6 6.9 %collective-permute-start.6 = (bf16[256,256]{1,0:T(8,128)(2,1)S(1)}, bf16[256,256]{1,0:T(8,128)(2,1)S(1)}, u32[]{:S(2)}, u32[]{:S(2)}) collective-permute-start(bf16[256,256]{1,0:T(8,128)(2,1)S(1)} %project.1), channel_id=1, source_target_pairs={{0,1},{1,0},{2,3},{3,2},{4,5},{5,4},{6,7},{7,6},{8,9},{9,8},{10,11... | collective-permute-start | bytes 393224 | tf_op jit(solution)/shard_map/ppermute | solution.py:388
  82.2 0.7 collective-permute-start.7
  82.9 25.5 %collective-permute-start.8 = (bf16[512,1536]{1,0:T(8,128)(2,1)S(1)}, bf16[512,1536]{1,0:T(8,128)(2,1)}, u32[]{:S(2)}, u32[]{:S(2)}) collective-permute-start(bf16[512,1536]{1,0:T(8,128)(2,1)S(1)} %bitcast.36), channel_id=1, source_target_pairs={{0,32},{32,0},{64,96},{96,64},{128,160},{160,128},{192,224},{224,1... | collective-permute-start | bytes 4718600 | tf_op jit(solution)/shard_map/ppermute | solution.py:366
  91.5 41.7 %all-to-all-start.1 = ((bf16[16,192,256]{2,1,0:T(8,128)(2,1)}), bf16[16,192,256]{2,1,0:T(8,128)(2,1)S(1)}, u32[]{:S(2)}, u32[]{:S(2)}) async-start(bf16[16,192,256]{2,1,0:T(8,128)(2,1)} %copy-done.2), calls=%async_computation.1 | async-start | bytes 3145728 | tf_op jit(solution)/shard_map/all_to_all | solution.py:398
  136.2 11.4 %collective-permute-start.10 = (bf16[96,1536]{1,0:T(8,128)(2,1)}, bf16[96,1536]{1,0:T(8,128)(2,1)S(1)}, u32[]{:S(2)}, u32[]{:S(2)}) collective-permute-start(bf16[96,1536]{1,0:T(8,128)(2,1)} %get-tuple-element.40), channel_id=1, source_target_pairs={{0,192},{32,224},{64,0},{96,32},{128,64},{160,96},{192,128},{224,1... | collective-permute-start | bytes 884744 | tf_op jit(solution)/shard_map/ppermute | solution.py:363
  137.4 10.5 %collective-permute-start.9 = (bf16[96,1536]{1,0:T(8,128)(2,1)}, bf16[96,1536]{1,0:T(8,128)(2,1)}, u32[]{:S(2)}, u32[]{:S(2)}) collective-permute-start(bf16[96,1536]{1,0:T(8,128)(2,1)} %get-tuple-element.39), channel_id=1, source_target_pairs={{0,64},{32,96},{64,128},{96,160},{128,192},{160,224},{192,0},{224,... | collective-permute-start | bytes 884744 | tf_op jit(solution)/shard_map/ppermute | solution.py:363
  150.5 31.8 %collective-permute-start.11 = (bf16[192,1536]{1,0:T(8,128)(2,1)}, bf16[192,1536]{1,0:T(8,128)(2,1)S(1)}, u32[]{:S(2)}, u32[]{:S(2)}) collective-permute-start(bf16[192,1536]{1,0:T(8,128)(2,1)} %pad_maximum_fusion.1), channel_id=1, source_target_pairs={{0,64},{32,96},{64,128},{96,160},{128,192},{160,224},{192,0},{224,... | collective-permute-start | bytes 1769480 | tf_op jit(solution)/shard_map/ppermute | solution.py:363
  151.9 30.3 %collective-permute-start.12 = (bf16[192,1536]{1,0:T(8,128)(2,1)S(1)}, bf16[192,1536]{1,0:T(8,128)(2,1)S(1)}, u32[]{:S(2)}, u32[]{:S(2)}) collective-permute-start(bf16[192,1536]{1,0:T(8,128)(2,1)S(1)} %pad_maximum_fusion.2), channel_id=1, source_target_pairs={{0,192},{32,224},{64,0},{96,32},{128,64},{160,96},{192,128},{224,1... | collective-permute-start | bytes 1769480 | tf_op jit(solution)/shard_map/ppermute | solution.py:363
  188.6 8.3 %copy-start.17 = (bf16[4,64,8]{1,2,0:T(8,128)(2,1)S(1)}, bf16[4,64,8]{1,2,0:T(8,128)(2,1)}, u32[]{:S(2)}) copy-start(bf16[4,64,8]{1,2,0:T(8,128)(2,1)} %param.23) | copy-start | bytes 12292
  188.6 25.6 %all-to-all-start.2 = ((bf16[16,192,256]{2,1,0:T(8,128)(2,1)}), bf16[16,192,256]{2,1,0:T(8,128)(2,1)S(1)}, u32[]{:S(2)}, u32[]{:S(2)}) async-start(bf16[16,192,256]{2,1,0:T(8,128)(2,1)} %contract.1), calls=%async_computation.2 | async-start | bytes 3145728 | tf_op jit(solution)/shard_map/all_to_all | solution.py:422
  196.9 32.1 %copy-start.13 = (bf16[256,256]{1,0:T(8,128)(2,1)S(1)}, bf16[256,256]{1,0:T(8,128)(2,1)}, u32[]{:S(2)}) copy-start(bf16[256,256]{1,0:T(8,128)(2,1)} %copy-done.12) | copy-start | bytes 393220
  216.2 12.8 %collective-permute-start.13 = (bf16[256,256]{1,0:T(8,128)(2,1)S(1)}, bf16[256,256]{1,0:T(8,128)(2,1)S(1)}, u32[]{:S(2)}, u32[]{:S(2)}) collective-permute-start(bf16[256,256]{1,0:T(8,128)(2,1)S(1)} %combine.1), channel_id=1, source_target_pairs={{0,1},{1,0},{2,3},{3,2},{4,5},{5,4},{6,7},{7,6},{8,9},{9,8},{10,11... | collective-permute-start | bytes 393224 | tf_op jit(solution)/shard_map/ppermute | solution.py:424
  (6 other events, 5.7 us)
Sparse Core Ops, SparseCore 0:
  25.1 56.5 all-gather.6
  83.5 55.4 all-gather.8

commit v3 on v2

--- a/solution.py
+++ b/solution.py
@@ -41,6 +41,10 @@
                     goal = ((y * 2 + c) * Y + z) * X + (x ^ (2 * c))
                     pairs.append((((z * 2 + c) * Y + y) * X + x, goal))
     return pairs
+
+
+def exchange(m):
+    return [(f, f ^ m) for f in range(Y * X)]
 
 
 def cost(us):
@@ -217,11 +221,12 @@
     high[...] = total[half:].astype(bf16)
 
 
-def expand_near_kernel(place, arrived, near, far, plus, minus, own):
+def expand_near_kernel(place, arrived, near, far, plus, plus_ready, minus_ready, minus, own):
     total = expand_rows(place, arrived, near, far, (1, 3, 0))
-    slots = own.shape[0]
-    for i, out in enumerate((plus, minus, own)):
-        out[...] = total[i * slots : (i + 1) * slots]
+    half = plus.shape[0]
+    for i, out in enumerate((plus, plus_ready, minus_ready, minus)):
+        out[...] = total[i * half : (i + 1) * half].astype(out.dtype)
+    own[...] = total[4 * half :]
 
 
 def expand_far(place, arrived, near, far):
@@ -241,17 +246,45 @@
     slots, width = arrived.shape[1], near.shape[2]
     return pl.pallas_call(
         expand_near_kernel,
-        out_shape=[jax.ShapeDtypeStruct((slots, width), f32)] * 3,
+        out_shape=[
+            jax.ShapeDtypeStruct((slots // 2, width), kind) for kind in (f32, bf16, bf16, f32)
+        ]
+        + [jax.ShapeDtypeStruct((slots, width), f32)],
         in_specs=[SMEM] + [VMEM] * 3,
-        out_specs=[VMEM] * 3,
+        out_specs=[VMEM] * 5,
         compiler_params=ROOM,
         cost_estimate=cost(4),
         name="expand_near",
     )(place, arrived, near, far)
 
 
-def contract_kernel(steps, place, ids, squares, own, one, two, *refs):
-    *weights, out = refs
+def contract_kernel(
+    steps,
+    place,
+    ids,
+    squares,
+    own,
+    plus,
+    plus_ready,
+    minus_ready,
+    minus,
+    first,
+    second,
+    out,
+    upper,
+    lower,
+    arrival,
+):
+    copies = [
+        [
+            pltpu.make_async_copy(whole.at[r], held.at[r], arrival.at[i, r])
+            for i, (whole, held) in enumerate(((first, upper), (second, lower)))
+        ]
+        for r in range(first.shape[0])
+    ]
+    for pair in copies:
+        for copy in pair:
+            copy.start()
     slots, width = out.shape[1:]
     half = own.shape[1] // 2
     top, rows = ids.shape
@@ -269,13 +302,19 @@
     slot_of = jnp.where(hit, iota((8, rows), 1) // block * CAP + rank - 1, -1)
     pick = slot_of[0:1, :] == iota((slots, rows), 0)
     slot_scale = jnp.sum(jnp.where(pick, row_scale, 0.0), axis=1, keepdims=True)
-    both = (own[...] + (one[...].astype(f32) + two[...].astype(f32))) * slot_scale
+    sums = [
+        first[...].astype(f32) + second[...].astype(f32)
+        for first, second in ((plus, minus_ready), (plus_ready, minus))
+    ]
+    both = (own[...] + jnp.concatenate(sums)) * slot_scale
     gate, up = both[:, :half], both[:, half:]
     hidden = (gate / (1.0 + jnp.exp(-gate)) * up).astype(bf16)
     split = half // 2
-    for r in range(weights[0].shape[0]):
-        result = jnp.dot(hidden[:, :split], weights[0][r], preferred_element_type=f32)
-        result = result + jnp.dot(hidden[:, split:], weights[1][r], preferred_element_type=f32)
+    for r, pair in enumerate(copies):
+        for copy in pair:
+            copy.wait()
+        result = jnp.dot(hidden[:, :split], upper[r], preferred_element_type=f32)
+        result = result + jnp.dot(hidden[:, split:], lower[r], preferred_element_type=f32)
         for i in range(2):
             out[2 * r + i] = result[:, i * width : (i + 1) * width].astype(bf16)
 
@@ -285,8 +324,13 @@
     return pl.pallas_call(
         functools.partial(contract_kernel, steps),
         out_shape=jax.ShapeDtypeStruct((experts, slots, width), bf16),
-        in_specs=[SMEM] + [VMEM] * (2 + len(parts) + len(weights)),
+        in_specs=[SMEM] + [VMEM] * (2 + len(parts)) + [ANY] * 2,
         out_specs=VMEM,
+        scratch_shapes=[
+            pltpu.VMEM(weights[0].shape, bf16),
+            pltpu.VMEM(weights[1].shape, bf16),
+            pltpu.SemaphoreType.DMA((2, weights[0].shape[0])),
+        ],
         compiler_params=ROOM,
         cost_estimate=cost(5),
         name="contract",
@@ -392,29 +436,34 @@
     scaled = (attended * norm_gain).astype(bf16)
     there = lax.ppermute(scaled, PLACES, swap_zy())
 
-    there, out_second = lax.optimization_barrier((there, out_second))
+    squares = jnp.sum(attended * attended, axis=-1).reshape(1, rows)
+    for m in (1, 2):
+        squares = squares + lax.ppermute(squares, "fsdp", exchange(m))
+
+    there, out_second, squares = lax.optimization_barrier((there, out_second, squares))
     out_second = lax.all_gather(out_second, "rep", axis=0, tiled=False)
     dispatched = dispatch(ids_there, there, experts, steps)
     arrived = lax.all_to_all(dispatched, "fsdp", split_axis=0, concat_axis=0, tiled=True)
 
+    for m in (4, 8):
+        squares = squares + lax.ppermute(squares, "fsdp", exchange(m))
+    arrived, squares = lax.optimization_barrier((arrived, squares))
+
     low, high = expand_far(place, arrived, near_in, far_in)
     low, high = shift(low, 1), shift(high, -1)
-    plus, minus, own = expand_near(place, arrived, near_in, far_in)
-    half = low.shape[0]
+    plus, plus_ready, minus_ready, minus, own = expand_near(place, arrived, near_in, far_in)
+    plus_ready, minus_ready = shift(plus_ready, 1), shift(minus_ready, -1)
     low, high, plus, minus = lax.optimization_barrier((low, high, plus, minus))
-    plus = jnp.concatenate([plus[:half] + low.astype(f32), plus[half:]]).astype(bf16)
-    minus = jnp.concatenate([minus[:half], minus[half:] + high.astype(f32)]).astype(bf16)
-    squares = jnp.sum(attended * attended, axis=-1).reshape(steps, block)
-    squares, plus, minus = lax.optimization_barrier((squares, plus, minus))
+    plus = (plus + low.astype(f32)).astype(bf16)
+    minus = (minus + high.astype(f32)).astype(bf16)
     plus, minus = shift(plus, 1), shift(minus, -1)
-    squares = lax.all_gather(squares, "fsdp", axis=0, tiled=False).reshape(experts, rows)
 
     result = contract(
         steps,
         place,
         ids_across,
         squares,
-        [own, plus, minus],
+        [own, plus, plus_ready, minus_ready, minus],
         [out_first, out_second],
         experts,
         model,

time: 238 us -> 235 us (0.987)
  blocking collectives: 27.5 us -> 0 us
  waiting for transfers between devices: 79.8 us -> 99.5 us
  starting transfers between devices: 76.4 us -> 81.4 us
  local copies, waits for them, and re-layouts: 10.3 us -> 14.4 us
  other arithmetic: 4.24 us -> 1.25 us
    all_gather x1 -> x0, blocking collectives: 27.5 us -> none  [on_device(): lax.all_gather(squares, 'fsdp', axis=0, tiled=False).reshape(experts, rows)]
    all_to_all x1, waiting for transfers between devices: 24.8 us -> 5.93 us  [on_device(): lax.all_to_all(dispatched, 'fsdp', split_axis=0, concat_axis=0, tiled=True)]
    ppermute x0 -> x4, waiting for transfers between devices: none -> 17.9 us  [on_device(): squares = squares + lax.ppermute(squares, 'fsdp', exchange(m))]
    ppermute x8 -> x10, waiting for transfers between devices: 9.66 us -> 20.2 us  [shift(): return lax.ppermute(value, 'rep', along_z(d))]
    ppermute x1, starting transfers between devices: 9.89 us -> 0.09 us  [on_device(): routed_cross = lax.ppermute(routed, 'tp', OTHER_HALF)]
    ppermute x0 -> x4, starting transfers between devices: none -> 9.68 us  [on_device(): squares = squares + lax.ppermute(squares, 'fsdp', exchange(m))]
    all_to_all x1, starting transfers between devices: 8.29 us -> 16.2 us  [on_device(): lax.all_to_all(result, 'fsdp', split_axis=0, concat_axis=0, tiled=True)]
    all_to_all x1, waiting for transfers between devices: 17.2 us -> 24.6 us  [on_device(): lax.all_to_all(result, 'fsdp', split_axis=0, concat_axis=0, tiled=True)]
  transfers between devices with their start and end apart: 19 -> 25, of which waited for: 10 -> 15; matrix products, arithmetic and copies ran while one was open for 3% -> 2% of each run, Pallas kernels for 7% -> 7%
where the time goes in v3:
time: 235 us
  waiting for transfers between devices  99.5 us (42%)
  starting transfers between devices  81.4 us (35%)
  Pallas kernels  24.4 us (10%)
  local copies, waits for them, and re-layouts  14.4 us (6%)
  between operations  13.8 us (6%)
    all_to_all x1, waiting for transfers between devices, on_device(): lax.all_to_all(result, 'fsdp', split_axis=0, concat_axis=0, tiled=True)  24.6 us
    ppermute x10, starting transfers between devices, shift(): return lax.ppermute(value, 'rep', along_z(d))  21.3 us
    ppermute x10, waiting for transfers between devices, shift(): return lax.ppermute(value, 'rep', along_z(d))  20.2 us
    all_to_all x1, waiting for transfers between devices, on_device(): attn = lax.all_to_all(attn, 'fsdp', split_axis=0, concat_axis=0, tiled=True)  19.9 us
    ppermute x4, waiting for transfers between devices, on_device(): squares = squares + lax.ppermute(squares, 'fsdp', exchange(m))  17.9 us
    all_to_all x1, starting transfers between devices, on_device(): lax.all_to_all(result, 'fsdp', split_axis=0, concat_axis=0, tiled=True)  16.2 us
    all_to_all x1, starting transfers between devices, on_device(): attn = lax.all_to_all(attn, 'fsdp', split_axis=0, concat_axis=0, tiled=True)  14.6 us
    all_to_all x1, starting transfers between devices, on_device(): lax.all_to_all(dispatched, 'fsdp', split_axis=0, concat_axis=0, tiled=True)  14.4 us
  transfers between devices with their start and end apart: 25, of which 15 were waited for; matrix products, arithmetic and copies ran while one was open for 2% of the time, Pallas kernels for 7%

profile of v3, /device:TPU:32, one launch (start us, length us, event | category | flops | bytes accessed | tf_op | source)
XLA Modules:
  0.0 234.7 jit_solution(15394624126296597180)
XLA Ops:
  6.6 3.3 %collective-permute-start.1 = (bf16[512,256]{1,0:T(8,128)(2,1)}, bf16[512,256]{1,0:T(8,128)(2,1)S(1)}, u32[]{:S(2)}, u32[]{:S(2)}) collective-permute-start(bf16[512,256]{1,0:T(8,128)(2,1)} %param.19), channel_id=1, source_target_pairs={{0,64},{32,96},{64,128},{96,160},{128,192},{160,224},{192,0},{224,... | collective-permute-start | bytes 786440 | tf_op jit(solution)/shard_map/ppermute | solution.py:407
  9.9 2.2 collective-permute-start.2
  13.6 2.1 slice_bitcast_fusion
  17.3 6.2 %attention.1 = bf16[16,16,4096]{2,1,0:T(8,128)(2,1)S(1)} custom-call(s32[4]{0:T(128)S(1)} %copy-done.14, bf16[4,4,4096]{2,1,0:T(4,128)(2,1)S(1)} %copy-done.11, bf16[4,1024,256]{2,1,0:T(8,128)(2,1)S(1)} %copy-done.2, bf16[4,1024,256]{2,1,0:T(8,128)(2,1)} %values.1, bf16[4,4,256]{2,1,0:T(4,128)(2,1)S(1)} %copy-done.12, bf16[4,4,256]{2,1,0:T(4,128)(2,1)S(1)} %copy-done.13), custom_call_target="tpu_custom_call" | custom-call | bytes 25200000 | tf_op jit(solution)/shard_map/attention/pallas_call | solution.py:128
  26.0 14.6 %all-to-all-start = ((bf16[16,16,4096]{2,1,0:T(8,128)(2,1)}), bf16[16,16,4096]{2,1,0:T(8,128)(2,1)}, u32[]{:S(2)}, u32[]{:S(2)}) async-start(bf16[16,16,4096]{2,1,0:T(8,128)(2,1)} %copy-done), calls=%async_computation | async-start | bytes 4194304 | tf_op jit(solution)/shard_map/all_to_all | solution.py:427
  40.7 2.4 %collective-permute-start.3 = (bf16[256,256]{1,0:T(8,128)(2,1)S(1)}, bf16[256,256]{1,0:T(8,128)(2,1)S(1)}, u32[]{:S(2)}, u32[]{:S(2)}) collective-permute-start(bf16[256,256]{1,0:T(8,128)(2,1)S(1)} %slice.13), channel_id=1, source_target_pairs={{0,64},{32,96},{64,128},{96,160},{128,192},{160,224},{192,0},{224,... | collective-permute-start | bytes 393224 | tf_op jit(solution)/shard_map/ppermute | solution.py:407
  43.1 1.9 collective-permute-start.4
  45.0 3.2 %collective-permute-done.3 = bf16[256,256]{1,0:T(8,128)(2,1)S(1)} collective-permute-done((bf16[256,256]{1,0:T(8,128)(2,1)S(1)}, bf16[256,256]{1,0:T(8,128)(2,1)S(1)}, u32[]{:S(2)}, u32[]{:S(2)}) %collective-permute-start.3) | collective-permute-done | bytes 131104 | tf_op jit(solution)/shard_map/ppermute | solution.py:407
  49.5 2.7 %collective-permute-done.5.theirs = bf16[4,512,256]{2,1,0:T(8,128)(2,1)} collective-permute-done((bf16[4,512,256]{2,1,0:T(8,128)(2,1)S(1)}, bf16[4,512,256]{2,1,0:T(8,128)(2,1)}, u32[]{:S(2)}, u32[]{:S(2)}) %collective-permute-start.5) | collective-permute-done | bytes 1048608 | tf_op jit(solution)/shard_map/ppermute | solution.py:410
  52.2 19.9 %all-to-all-done = bf16[16,16,4096]{2,1,0:T(8,128)(2,1)} async-done(((bf16[16,16,4096]{2,1,0:T(8,128)(2,1)}), bf16[16,16,4096]{2,1,0:T(8,128)(2,1)}, u32[]{:S(2)}, u32[]{:S(2)}) %all-to-all-start) | async-done | bytes 2097184 | tf_op jit(solution)/shard_map/all_to_all | solution.py:427
  72.0 2.7 %project.1 = bf16[256,256]{1,0:T(8,128)(2,1)S(1)} custom-call(s32[4]{0:T(128)S(1)} %pad_add_fusion.place, bf16[256,4096]{1,0:T(8,128)(2,1)} %bitcast.12.attn, bf16[4,512,256]{2,1,0:T(8,128)(2,1)S(1)} %pad_maximum_fusion.mine, bf16[4,512,256]{2,1,0:T(8,128)(2,1)} %collective-permute-done.5.theirs), custom_call_target="tpu_custom_call" | custom-call | bytes 10800000 | tf_op jit(solution)/shard_map/project/pallas_call | solution.py:164
  76.4 3.4 %collective-permute-done.6 = bf16[256,256]{1,0:T(8,128)(2,1)S(1)} collective-permute-done((bf16[256,256]{1,0:T(8,128)(2,1)S(1)}, bf16[256,256]{1,0:T(8,128)(2,1)S(1)}, u32[]{:S(2)}, u32[]{:S(2)}) %collective-permute-start.6) | collective-permute-done | bytes 131104 | tf_op jit(solution)/shard_map/ppermute | solution.py:432
  84.3 3.2 %collective-permute-start.9 = (f32[1,256]{1,0:T(1,128)S(1)}, f32[1,256]{1,0:T(1,128)S(1)}, u32[]{:S(2)}, u32[]{:S(2)}) collective-permute-start(f32[1,256]{1,0:T(1,128)S(1)} %add.38), channel_id=1, source_target_pairs={{0,4},{2,6},{4,0},{6,2},{8,12},{10,14},{12,8},{14,10},{16,20},{18,... | collective-permute-start | bytes 3080 | tf_op jit(solution)/shard_map/ppermute | solution.py:441
  89.4 1.9 collective-permute-start.12
  93.4 14.4 %all-to-all-start.1 = ((bf16[16,192,256]{2,1,0:T(8,128)(2,1)}), bf16[16,192,256]{2,1,0:T(8,128)(2,1)S(1)}, u32[]{:S(2)}, u32[]{:S(2)}) async-start(bf16[16,192,256]{2,1,0:T(8,128)(2,1)} %copy-done.1), calls=%async_computation.1 | async-start | bytes 3145728 | tf_op jit(solution)/shard_map/all_to_all | solution.py:446
  107.8 1.9 collective-permute-start.10
  109.7 9.4 %collective-permute-done.10 = f32[1,256]{1,0:T(1,128)S(1)} collective-permute-done((f32[1,256]{1,0:T(1,128)S(1)}, f32[1,256]{1,0:T(1,128)S(1)}, u32[]{:S(2)}, u32[]{:S(2)}) %collective-permute-start.10) | collective-permute-done | bytes 1056 | tf_op jit(solution)/shard_map/ppermute | solution.py:449
  119.1 2.7 %collective-permute-start.11 = (f32[1,256]{1,0:T(1,128)S(1)}, f32[1,256]{1,0:T(1,128)S(1)}, u32[]{:S(2)}, u32[]{:S(2)}) collective-permute-start(f32[1,256]{1,0:T(1,128)S(1)} %add.40), channel_id=1, source_target_pairs={{0,16},{2,18},{4,20},{6,22},{8,24},{10,26},{12,28},{14,30},{16,0},... | collective-permute-start | bytes 3080 | tf_op jit(solution)/shard_map/ppermute | solution.py:449
  121.8 4.8 %collective-permute-done.11 = f32[1,256]{1,0:T(1,128)S(1)} collective-permute-done((f32[1,256]{1,0:T(1,128)S(1)}, f32[1,256]{1,0:T(1,128)S(1)}, u32[]{:S(2)}, u32[]{:S(2)}) %collective-permute-start.11) | collective-permute-done | bytes 1056 | tf_op jit(solution)/shard_map/ppermute | solution.py:449
  126.7 5.9 %all-to-all-done.1.arrived = bf16[16,192,256]{2,1,0:T(8,128)(2,1)S(1)} async-done(((bf16[16,192,256]{2,1,0:T(8,128)(2,1)}), bf16[16,192,256]{2,1,0:T(8,128)(2,1)S(1)}, u32[]{:S(2)}, u32[]{:S(2)}) %all-to-all-start.1) | async-done | bytes 1572896 | tf_op jit(solution)/shard_map/all_to_all | solution.py:446
  132.6 2.2 expand_far.1
  135.3 3.7 %collective-permute-start.14 = (bf16[96,1536]{1,0:T(8,128)(2,1)S(1)}, bf16[96,1536]{1,0:T(8,128)(2,1)S(1)}, u32[]{:S(2)}, u32[]{:S(2)}) collective-permute-start(bf16[96,1536]{1,0:T(8,128)(2,1)S(1)} %get-tuple-element.46), channel_id=1, source_target_pairs={{0,192},{32,224},{64,0},{96,32},{128,64},{160,96},{192,128},{224,1... | collective-permute-start | bytes 884744 | tf_op jit(solution)/shard_map/ppermute | solution.py:407
  139.0 4.2 %expand_near.1 = (f32[96,1536]{1,0:T(8,128)S(1)}, bf16[96,1536]{1,0:T(8,128)(2,1)}, bf16[96,1536]{1,0:T(8,128)(2,1)}, f32[96,1536]{1,0:T(8,128)S(1)}, f32[192,1536]{1,0:T(8,128)S(1)}) custom-call(s32[4]{0:T(128)S(1)} %pad_add_fusion.place, bf16[16,192,256]{2,1,0:T(8,128)(2,1)S(1)} %all-to-all-done.1.arrived, bf16[2,256,1536]{2,1,0:T(8,128)(2,1)S(1)} %bitcast.38, ...), custom_call_target="tpu_custom_call" | custom-call | bytes 14400000 | tf_op jit(solution)/shard_map/expand_near/pallas_call | solution.py:247
  144.3 4.1 %collective-permute-start.17 = (bf16[96,1536]{1,0:T(8,128)(2,1)}, bf16[96,1536]{1,0:T(8,128)(2,1)S(1)}, u32[]{:S(2)}, u32[]{:S(2)}) collective-permute-start(bf16[96,1536]{1,0:T(8,128)(2,1)} %get-tuple-element.52), channel_id=1, source_target_pairs={{0,192},{32,224},{64,0},{96,32},{128,64},{160,96},{192,128},{224,1... | collective-permute-start | bytes 884744 | tf_op jit(solution)/shard_map/ppermute | solution.py:407
  148.4 4.8 %collective-permute-done.13 = bf16[96,1536]{1,0:T(8,128)(2,1)S(1)} collective-permute-done((bf16[96,1536]{1,0:T(8,128)(2,1)S(1)}, bf16[96,1536]{1,0:T(8,128)(2,1)S(1)}, u32[]{:S(2)}, u32[]{:S(2)}) %collective-permute-start.13) | collective-permute-done | bytes 294944 | tf_op jit(solution)/shard_map/ppermute | solution.py:407
  156.5 5.3 %collective-permute-done.16.plus_ready = bf16[96,1536]{1,0:T(8,128)(2,1)S(1)} collective-permute-done((bf16[96,1536]{1,0:T(8,128)(2,1)}, bf16[96,1536]{1,0:T(8,128)(2,1)S(1)}, u32[]{:S(2)}, u32[]{:S(2)}) %collective-permute-start.16) | collective-permute-done | bytes 294944 | tf_op jit(solution)/shard_map/ppermute | solution.py:407
  162.6 5.9 %collective-permute-done.18.minus = bf16[96,1536]{1,0:T(8,128)(2,1)S(1)} collective-permute-done((bf16[96,1536]{1,0:T(8,128)(2,1)S(1)}, bf16[96,1536]{1,0:T(8,128)(2,1)S(1)}, u32[]{:S(2)}, u32[]{:S(2)}) %collective-permute-start.18) | collective-permute-done | bytes 294944 | tf_op jit(solution)/shard_map/ppermute | solution.py:407
  172.9 6.3 %contract.1 = bf16[16,192,256]{2,1,0:T(8,128)(2,1)} custom-call(s32[4]{0:T(128)S(1)} %pad_add_fusion.place, s32[8,256]{1,0:T(8,128)S(1)} %copy.17.ids, f32[1,256]{1,0:T(1,128)S(1)} %add.41.squares, f32[192,1536]{1,0:T(8,128)S(1)} %copy-done.4, bf16[96,1536]{1,0:T(8,128)(2,1)S(1)} %copy-done.10, bf16[96,1536]{1,0:T(8,128)(2,1)S(1)} %collective-permute-done.16.plus_ready, ...), custom_call_target="tpu_custom_call" | custom-call | bytes 18000000 | tf_op jit(solution)/shard_map/contract/pallas_call | solution.py:324
  179.2 16.2 %all-to-all-start.2 = ((bf16[16,192,256]{2,1,0:T(8,128)(2,1)}), bf16[16,192,256]{2,1,0:T(8,128)(2,1)S(1)}, u32[]{:S(2)}, u32[]{:S(2)}) async-start(bf16[16,192,256]{2,1,0:T(8,128)(2,1)} %contract.1), calls=%async_computation.2 | async-start | bytes 3145728 | tf_op jit(solution)/shard_map/all_to_all | solution.py:471
  195.5 24.6 %all-to-all-done.2.refs_0_ = bf16[16,192,256]{2,1,0:T(8,128)(2,1)S(1)} async-done(((bf16[16,192,256]{2,1,0:T(8,128)(2,1)}), bf16[16,192,256]{2,1,0:T(8,128)(2,1)S(1)}, u32[]{:S(2)}, u32[]{:S(2)}) %all-to-all-start.2) | async-done | bytes 1572896 | tf_op jit(solution)/shard_map/all_to_all | solution.py:471
  220.1 2.0 combine.1
  222.2 5.0 %collective-permute-done.19 = bf16[256,256]{1,0:T(8,128)(2,1)S(1)} collective-permute-done((bf16[256,256]{1,0:T(8,128)(2,1)S(1)}, bf16[256,256]{1,0:T(8,128)(2,1)S(1)}, u32[]{:S(2)}, u32[]{:S(2)}) %collective-permute-start.19) | collective-permute-done | bytes 131104 | tf_op jit(solution)/shard_map/ppermute | solution.py:473
  (102 shorter events, 27.6 us)
Async XLA Ops:
  6.5 163.4 %all-gather.5.cloned.1.call-start = ((), (), s32[]{:S(2)}) async-start(), calls=%async_computation.3 | async-start | bytes 3538944 | tf_op jit(solution)/shard_map/all_gather | solution.py:420
  6.6 18.3 %collective-permute-start.1 = (bf16[512,256]{1,0:T(8,128)(2,1)}, bf16[512,256]{1,0:T(8,128)(2,1)S(1)}, u32[]{:S(2)}, u32[]{:S(2)}) collective-permute-start(bf16[512,256]{1,0:T(8,128)(2,1)} %param.19), channel_id=1, source_target_pairs={{0,64},{32,96},{64,128},{96,160},{128,192},{160,224},{192,0},{224,... | collective-permute-start | bytes 786440 | tf_op jit(solution)/shard_map/ppermute | solution.py:407
  9.9 15.0 %collective-permute-start.2 = (bf16[512,256]{1,0:T(8,128)(2,1)}, bf16[512,256]{1,0:T(8,128)(2,1)S(1)}, u32[]{:S(2)}, u32[]{:S(2)}) collective-permute-start(bf16[512,256]{1,0:T(8,128)(2,1)} %param.19), channel_id=1, source_target_pairs={{0,192},{32,224},{64,0},{96,32},{128,64},{160,96},{192,128},{224,1... | collective-permute-start | bytes 786440 | tf_op jit(solution)/shard_map/ppermute | solution.py:407
  13.0 11.9 %collective-permute-start = (s32[8,256]{0,1:T(8,128)S(1)}, s32[8,256]{0,1:T(8,128)S(1)}, u32[]{:S(2)}, u32[]{:S(2)}) collective-permute-start(s32[8,256]{0,1:T(8,128)S(1)} %bitcast.39), channel_id=1, source_target_pairs={{0,0},{2,2},{4,4},{6,6},{8,64},{10,66},{12,68},{14,70},{16,128},{1... | collective-permute-start | bytes 24584 | tf_op jit(solution)/shard_map/ppermute | solution.py:413
  26.0 14.7 %copy-start.17 = (bf16[512,256]{1,0:T(8,128)(2,1)S(1)}, bf16[512,256]{1,0:T(8,128)(2,1)}, u32[]{:S(2)}) copy-start(bf16[512,256]{1,0:T(8,128)(2,1)} %copy-done.16) | copy-start | bytes 786436
  26.0 17.1 %copy-start.19 = (bf16[512,256]{1,0:T(8,128)(2,1)S(1)}, bf16[512,256]{1,0:T(8,128)(2,1)}, u32[]{:S(2)}) copy-start(bf16[512,256]{1,0:T(8,128)(2,1)} %copy-done.18) | copy-start | bytes 786436
  26.0 23.1 %copy-start.23 = (bf16[512,256]{1,0:T(8,128)(2,1)S(1)}, bf16[512,256]{1,0:T(8,128)(2,1)}, u32[]{:S(2)}) copy-start(bf16[512,256]{1,0:T(8,128)(2,1)} %param.19) | copy-start | bytes 786436
  26.0 46.0 %all-to-all-start = ((bf16[16,16,4096]{2,1,0:T(8,128)(2,1)}), bf16[16,16,4096]{2,1,0:T(8,128)(2,1)}, u32[]{:S(2)}, u32[]{:S(2)}) async-start(bf16[16,16,4096]{2,1,0:T(8,128)(2,1)} %copy-done), calls=%async_computation | async-start | bytes 4194304 | tf_op jit(solution)/shard_map/all_to_all | solution.py:427
  40.6 129.3 %all-gather.7.cloned.1.call-start = ((), (), s32[]{:S(2)}) async-start(), calls=%async_computation.4 | async-start | bytes 3538944 | tf_op jit(solution)/shard_map/all_gather | solution.py:444
  40.7 7.5 %collective-permute-start.3 = (bf16[256,256]{1,0:T(8,128)(2,1)S(1)}, bf16[256,256]{1,0:T(8,128)(2,1)S(1)}, u32[]{:S(2)}, u32[]{:S(2)}) collective-permute-start(bf16[256,256]{1,0:T(8,128)(2,1)S(1)} %slice.13), channel_id=1, source_target_pairs={{0,64},{32,96},{64,128},{96,160},{128,192},{160,224},{192,0},{224,... | collective-permute-start | bytes 393224 | tf_op jit(solution)/shard_map/ppermute | solution.py:407
  43.1 6.0 %collective-permute-start.4 = (bf16[256,256]{1,0:T(8,128)(2,1)S(1)}, bf16[256,256]{1,0:T(8,128)(2,1)S(1)}, u32[]{:S(2)}, u32[]{:S(2)}) collective-permute-start(bf16[256,256]{1,0:T(8,128)(2,1)S(1)} %slice.14), channel_id=1, source_target_pairs={{0,192},{32,224},{64,0},{96,32},{128,64},{160,96},{192,128},{224,1... | collective-permute-start | bytes 393224 | tf_op jit(solution)/shard_map/ppermute | solution.py:407
  49.3 2.9 %collective-permute-start.5 = (bf16[4,512,256]{2,1,0:T(8,128)(2,1)S(1)}, bf16[4,512,256]{2,1,0:T(8,128)(2,1)}, u32[]{:S(2)}, u32[]{:S(2)}) collective-permute-start(bf16[4,512,256]{2,1,0:T(8,128)(2,1)S(1)} %pad_maximum_fusion.mine), channel_id=1, source_target_pairs={{0,32},{32,0},{64,96},{96,64},{128,160},{160,128},{192,224},{224,1... | collective-permute-start | bytes 3145736 | tf_op jit(solution)/shard_map/ppermute | solution.py:410
  72.0 19.4 %copy-start.25 = (s32[8,256]{0,1:T(8,128)S(1)}, s32[8,256]{0,1:T(8,128)}, u32[]{:S(2)}) copy-start(s32[8,256]{0,1:T(8,128)} %copy-done.24) | copy-start | bytes 24580
  74.8 5.1 %collective-permute-start.6 = (bf16[256,256]{1,0:T(8,128)(2,1)S(1)}, bf16[256,256]{1,0:T(8,128)(2,1)S(1)}, u32[]{:S(2)}, u32[]{:S(2)}) collective-permute-start(bf16[256,256]{1,0:T(8,128)(2,1)S(1)} %project.1), channel_id=1, source_target_pairs={{0,1},{1,0},{2,3},{3,2},{4,5},{5,4},{6,7},{7,6},{8,9},{9,8},{10,11... | collective-permute-start | bytes 393224 | tf_op jit(solution)/shard_map/ppermute | solution.py:432
  80.0 9.4 %collective-permute-start.7 = (bf16[256,256]{1,0:T(8,128)(2,1)S(1)}, bf16[256,256]{1,0:T(8,128)(2,1)S(1)}, u32[]{:S(2)}, u32[]{:S(2)}) collective-permute-start(bf16[256,256]{1,0:T(8,128)(2,1)S(1)} %get-tuple-element.60), channel_id=1, source_target_pairs={{0,0},{2,2},{4,4},{6,6},{8,64},{10,66},{12,68},{14,70},{16,128},{1... | collective-permute-start | bytes 393224 | tf_op jit(solution)/shard_map/ppermute | solution.py:437
  80.7 3.7 %collective-permute-start.8 = (f32[1,256]{1,0:T(1,128)S(1)}, f32[1,256]{1,0:T(1,128)S(1)}, u32[]{:S(2)}, u32[]{:S(2)}) collective-permute-start(f32[1,256]{1,0:T(1,128)S(1)} %bitcast.49), channel_id=1, source_target_pairs={{0,2},{2,0},{4,6},{6,4},{8,10},{10,8},{12,14},{14,12},{16,18},{18,... | collective-permute-start | bytes 3080 | tf_op jit(solution)/shard_map/ppermute | solution.py:441
  84.3 5.1 %collective-permute-start.9 = (f32[1,256]{1,0:T(1,128)S(1)}, f32[1,256]{1,0:T(1,128)S(1)}, u32[]{:S(2)}, u32[]{:S(2)}) collective-permute-start(f32[1,256]{1,0:T(1,128)S(1)} %add.38), channel_id=1, source_target_pairs={{0,4},{2,6},{4,0},{6,2},{8,12},{10,14},{12,8},{14,10},{16,20},{18,... | collective-permute-start | bytes 3080 | tf_op jit(solution)/shard_map/ppermute | solution.py:441
  89.4 43.2 %collective-permute-start.12 = (bf16[512,1536]{1,0:T(8,128)(2,1)S(1)}, bf16[512,1536]{1,0:T(8,128)(2,1)}, u32[]{:S(2)}, u32[]{:S(2)}) collective-permute-start(bf16[512,1536]{1,0:T(8,128)(2,1)S(1)} %bitcast.36), channel_id=1, source_target_pairs={{0,32},{32,0},{64,96},{96,64},{128,160},{160,128},{192,224},{224,1... | collective-permute-start | bytes 4718600 | tf_op jit(solution)/shard_map/ppermute | solution.py:410
  93.4 39.2 %all-to-all-start.1 = ((bf16[16,192,256]{2,1,0:T(8,128)(2,1)}), bf16[16,192,256]{2,1,0:T(8,128)(2,1)S(1)}, u32[]{:S(2)}, u32[]{:S(2)}) async-start(bf16[16,192,256]{2,1,0:T(8,128)(2,1)} %copy-done.1), calls=%async_computation.1 | async-start | bytes 3145728 | tf_op jit(solution)/shard_map/all_to_all | solution.py:446
  107.8 11.3 %collective-permute-start.10 = (f32[1,256]{1,0:T(1,128)S(1)}, f32[1,256]{1,0:T(1,128)S(1)}, u32[]{:S(2)}, u32[]{:S(2)}) collective-permute-start(f32[1,256]{1,0:T(1,128)S(1)} %add.39), channel_id=1, source_target_pairs={{0,8},{2,10},{4,12},{6,14},{8,0},{10,2},{12,4},{14,6},{16,24},{18,... | collective-permute-start | bytes 3080 | tf_op jit(solution)/shard_map/ppermute | solution.py:449
  119.1 7.5 %collective-permute-start.11 = (f32[1,256]{1,0:T(1,128)S(1)}, f32[1,256]{1,0:T(1,128)S(1)}, u32[]{:S(2)}, u32[]{:S(2)}) collective-permute-start(f32[1,256]{1,0:T(1,128)S(1)} %add.40), channel_id=1, source_target_pairs={{0,16},{2,18},{4,20},{6,22},{8,24},{10,26},{12,28},{14,30},{16,0},... | collective-permute-start | bytes 3080 | tf_op jit(solution)/shard_map/ppermute | solution.py:449
  134.8 18.4 %collective-permute-start.13 = (bf16[96,1536]{1,0:T(8,128)(2,1)S(1)}, bf16[96,1536]{1,0:T(8,128)(2,1)S(1)}, u32[]{:S(2)}, u32[]{:S(2)}) collective-permute-start(bf16[96,1536]{1,0:T(8,128)(2,1)S(1)} %get-tuple-element.45), channel_id=1, source_target_pairs={{0,64},{32,96},{64,128},{96,160},{128,192},{160,224},{192,0},{224,... | collective-permute-start | bytes 884744 | tf_op jit(solution)/shard_map/ppermute | solution.py:407
  135.3 17.9 %collective-permute-start.14 = (bf16[96,1536]{1,0:T(8,128)(2,1)S(1)}, bf16[96,1536]{1,0:T(8,128)(2,1)S(1)}, u32[]{:S(2)}, u32[]{:S(2)}) collective-permute-start(bf16[96,1536]{1,0:T(8,128)(2,1)S(1)} %get-tuple-element.46), channel_id=1, source_target_pairs={{0,192},{32,224},{64,0},{96,32},{128,64},{160,96},{192,128},{224,1... | collective-permute-start | bytes 884744 | tf_op jit(solution)/shard_map/ppermute | solution.py:407
  144.3 25.7 %copy-start.4 = (f32[192,1536]{1,0:T(8,128)S(1)}, f32[192,1536]{1,0:T(8,128)}, u32[]{:S(2)}) copy-start(f32[192,1536]{1,0:T(8,128)} %copy-done.3) | copy-start | bytes 3538948
  144.3 17.5 %collective-permute-start.16 = (bf16[96,1536]{1,0:T(8,128)(2,1)}, bf16[96,1536]{1,0:T(8,128)(2,1)S(1)}, u32[]{:S(2)}, u32[]{:S(2)}) collective-permute-start(bf16[96,1536]{1,0:T(8,128)(2,1)} %get-tuple-element.51), channel_id=1, source_target_pairs={{0,64},{32,96},{64,128},{96,160},{128,192},{160,224},{192,0},{224,... | collective-permute-start | bytes 884744 | tf_op jit(solution)/shard_map/ppermute | solution.py:407
  144.3 17.5 %collective-permute-start.17 = (bf16[96,1536]{1,0:T(8,128)(2,1)}, bf16[96,1536]{1,0:T(8,128)(2,1)S(1)}, u32[]{:S(2)}, u32[]{:S(2)}) collective-permute-start(bf16[96,1536]{1,0:T(8,128)(2,1)} %get-tuple-element.52), channel_id=1, source_target_pairs={{0,192},{32,224},{64,0},{96,32},{128,64},{160,96},{192,128},{224,1... | collective-permute-start | bytes 884744 | tf_op jit(solution)/shard_map/ppermute | solution.py:407
  153.3 15.2 %collective-permute-start.18 = (bf16[96,1536]{1,0:T(8,128)(2,1)S(1)}, bf16[96,1536]{1,0:T(8,128)(2,1)S(1)}, u32[]{:S(2)}, u32[]{:S(2)}) collective-permute-start(bf16[96,1536]{1,0:T(8,128)(2,1)S(1)} %add_convert_fusion), channel_id=1, source_target_pairs={{0,192},{32,224},{64,0},{96,32},{128,64},{160,96},{192,128},{224,1... | collective-permute-start | bytes 884744 | tf_op jit(solution)/shard_map/ppermute | solution.py:407
  155.2 14.0 %collective-permute-start.15 = (bf16[96,1536]{1,0:T(8,128)(2,1)S(1)}, bf16[96,1536]{1,0:T(8,128)(2,1)S(1)}, u32[]{:S(2)}, u32[]{:S(2)}) collective-permute-start(bf16[96,1536]{1,0:T(8,128)(2,1)S(1)} %add_convert_fusion.1), channel_id=1, source_target_pairs={{0,64},{32,96},{64,128},{96,160},{128,192},{160,224},{192,0},{224,... | collective-permute-start | bytes 884744 | tf_op jit(solution)/shard_map/ppermute | solution.py:407
  179.1 16.2 %copy-start.26 = (bf16[4,64,8]{1,2,0:T(8,128)(2,1)S(1)}, bf16[4,64,8]{1,2,0:T(8,128)(2,1)}, u32[]{:S(2)}) copy-start(bf16[4,64,8]{1,2,0:T(8,128)(2,1)} %param.23) | copy-start | bytes 12292
  179.2 40.9 %all-to-all-start.2 = ((bf16[16,192,256]{2,1,0:T(8,128)(2,1)}), bf16[16,192,256]{2,1,0:T(8,128)(2,1)S(1)}, u32[]{:S(2)}, u32[]{:S(2)}) async-start(bf16[16,192,256]{2,1,0:T(8,128)(2,1)} %contract.1), calls=%async_computation.2 | async-start | bytes 3145728 | tf_op jit(solution)/shard_map/all_to_all | solution.py:471
  195.4 31.8 %copy-start.22 = (bf16[256,256]{1,0:T(8,128)(2,1)S(1)}, bf16[256,256]{1,0:T(8,128)(2,1)}, u32[]{:S(2)}) copy-start(bf16[256,256]{1,0:T(8,128)(2,1)} %copy-done.21) | copy-start | bytes 393220
  222.1 5.1 %collective-permute-start.19 = (bf16[256,256]{1,0:T(8,128)(2,1)S(1)}, bf16[256,256]{1,0:T(8,128)(2,1)S(1)}, u32[]{:S(2)}, u32[]{:S(2)}) collective-permute-start(bf16[256,256]{1,0:T(8,128)(2,1)S(1)} %combine.1), channel_id=1, source_target_pairs={{0,1},{1,0},{2,3},{3,2},{4,5},{5,4},{6,7},{7,6},{8,9},{9,8},{10,11... | collective-permute-start | bytes 393224 | tf_op jit(solution)/shard_map/ppermute | solution.py:473
  (21 other events, 82.8 us)
Sparse Core Ops, SparseCore 0:
  25.1 54.9 all-gather.4
  89.6 48.0 all-gather.6

commit v4 on v3

--- a/solution.py
+++ b/solution.py
@@ -263,18 +263,17 @@
     place,
     ids,
     squares,
-    own,
-    plus,
-    plus_ready,
-    minus_ready,
-    minus,
-    first,
-    second,
-    out,
-    upper,
-    lower,
-    arrival,
+    *refs,
 ):
+    sent, (first, second, out), held_parts = refs[:5], refs[5:8], refs[8:13]
+    upper, lower, arrival, part_arrival = refs[13:]
+    own, plus, plus_ready, minus_ready, minus = held_parts
+    part_copies = [
+        pltpu.make_async_copy(whole, held, part_arrival.at[i])
+        for i, (whole, held) in enumerate(zip(sent, held_parts))
+    ]
+    for copy in part_copies:
+        copy.start()
     copies = [
         [
             pltpu.make_async_copy(whole.at[r], held.at[r], arrival.at[i, r])
@@ -302,9 +301,11 @@
     slot_of = jnp.where(hit, iota((8, rows), 1) // block * CAP + rank - 1, -1)
     pick = slot_of[0:1, :] == iota((slots, rows), 0)
     slot_scale = jnp.sum(jnp.where(pick, row_scale, 0.0), axis=1, keepdims=True)
+    for copy in part_copies:
+        copy.wait()
     sums = [
-        first[...].astype(f32) + second[...].astype(f32)
-        for first, second in ((plus, minus_ready), (plus_ready, minus))
+        one[...].astype(f32) + two[...].astype(f32)
+        for one, two in ((plus, minus_ready), (plus_ready, minus))
     ]
     both = (own[...] + jnp.concatenate(sums)) * slot_scale
     gate, up = both[:, :half], both[:, half:]
@@ -324,12 +325,14 @@
     return pl.pallas_call(
         functools.partial(contract_kernel, steps),
         out_shape=jax.ShapeDtypeStruct((experts, slots, width), bf16),
-        in_specs=[SMEM] + [VMEM] * (2 + len(parts)) + [ANY] * 2,
+        in_specs=[SMEM] + [VMEM] * 2 + [ANY] * (len(parts) + 2),
         out_specs=VMEM,
-        scratch_shapes=[
+        scratch_shapes=[pltpu.VMEM(part.shape, part.dtype) for part in parts]
+        + [
             pltpu.VMEM(weights[0].shape, bf16),
             pltpu.VMEM(weights[1].shape, bf16),
             pltpu.SemaphoreType.DMA((2, weights[0].shape[0])),
+            pltpu.SemaphoreType.DMA((len(parts),)),
         ],
         compiler_params=ROOM,
         cost_estimate=cost(5),

time: 235 us -> 236 us (level)
  no operation moved by 1% of the time
where the time goes in v4:
time: 236 us; the launch traced here: 235 us
  waiting for transfers between devices  99.5 us (42%)
  starting transfers between devices  81.4 us (34%)
  Pallas kernels  24.7 us (10%)
  local copies, waits for them, and re-layouts  14.4 us (6%)
  between operations  13.8 us (6%)
    all_to_all x1, waiting for transfers between devices, on_device(): lax.all_to_all(result, 'fsdp', split_axis=0, concat_axis=0, tiled=True)  24.6 us
    ppermute x10, starting transfers between devices, shift(): return lax.ppermute(value, 'rep', along_z(d))  21.3 us
    ppermute x10, waiting for transfers between devices, shift(): return lax.ppermute(value, 'rep', along_z(d))  20.2 us
    all_to_all x1, waiting for transfers between devices, on_device(): attn = lax.all_to_all(attn, 'fsdp', split_axis=0, concat_axis=0, tiled=True)  19.9 us
    ppermute x4, waiting for transfers between devices, on_device(): squares = squares + lax.ppermute(squares, 'fsdp', exchange(m))  17.9 us
    all_to_all x1, starting transfers between devices, on_device(): lax.all_to_all(result, 'fsdp', split_axis=0, concat_axis=0, tiled=True)  16.2 us
    all_to_all x1, starting transfers between devices, on_device(): attn = lax.all_to_all(attn, 'fsdp', split_axis=0, concat_axis=0, tiled=True)  14.6 us
    all_to_all x1, starting transfers between devices, on_device(): lax.all_to_all(dispatched, 'fsdp', split_axis=0, concat_axis=0, tiled=True)  14.4 us
  transfers between devices with their start and end apart: 25, of which 15 were waited for; matrix products, arithmetic and copies ran while one was open for 2% of the time, Pallas kernels for 7%

profile of v4, /device:TPU:32, one launch (start us, length us, event | category | flops | bytes accessed | tf_op | source)
XLA Modules:
  0.0 235.0 jit_solution(17845535029617005305)
XLA Ops:
  6.6 3.3 %collective-permute-start.1 = (bf16[512,256]{1,0:T(8,128)(2,1)}, bf16[512,256]{1,0:T(8,128)(2,1)S(1)}, u32[]{:S(2)}, u32[]{:S(2)}) collective-permute-start(bf16[512,256]{1,0:T(8,128)(2,1)} %param.19), channel_id=1, source_target_pairs={{0,64},{32,96},{64,128},{96,160},{128,192},{160,224},{192,0},{224,... | collective-permute-start | bytes 786440 | tf_op jit(solution)/shard_map/ppermute | solution.py:410
  9.9 2.2 collective-permute-start.2
  13.6 2.1 slice_bitcast_fusion
  17.3 6.2 %attention.1 = bf16[16,16,4096]{2,1,0:T(8,128)(2,1)S(1)} custom-call(s32[4]{0:T(128)S(1)} %copy-done.14, bf16[4,4,4096]{2,1,0:T(4,128)(2,1)S(1)} %copy-done.11, bf16[4,1024,256]{2,1,0:T(8,128)(2,1)S(1)} %copy-done.2, bf16[4,1024,256]{2,1,0:T(8,128)(2,1)} %values.1, bf16[4,4,256]{2,1,0:T(4,128)(2,1)S(1)} %copy-done.12, bf16[4,4,256]{2,1,0:T(4,128)(2,1)S(1)} %copy-done.13), custom_call_target="tpu_custom_call" | custom-call | bytes 25200000 | tf_op jit(solution)/shard_map/attention/pallas_call | solution.py:128
  26.0 14.6 %all-to-all-start = ((bf16[16,16,4096]{2,1,0:T(8,128)(2,1)}), bf16[16,16,4096]{2,1,0:T(8,128)(2,1)}, u32[]{:S(2)}, u32[]{:S(2)}) async-start(bf16[16,16,4096]{2,1,0:T(8,128)(2,1)} %copy-done), calls=%async_computation | async-start | bytes 4194304 | tf_op jit(solution)/shard_map/all_to_all | solution.py:430
  40.7 2.4 %collective-permute-start.3 = (bf16[256,256]{1,0:T(8,128)(2,1)S(1)}, bf16[256,256]{1,0:T(8,128)(2,1)S(1)}, u32[]{:S(2)}, u32[]{:S(2)}) collective-permute-start(bf16[256,256]{1,0:T(8,128)(2,1)S(1)} %slice.13), channel_id=1, source_target_pairs={{0,64},{32,96},{64,128},{96,160},{128,192},{160,224},{192,0},{224,... | collective-permute-start | bytes 393224 | tf_op jit(solution)/shard_map/ppermute | solution.py:410
  43.1 1.9 collective-permute-start.4
  45.0 3.2 %collective-permute-done.3 = bf16[256,256]{1,0:T(8,128)(2,1)S(1)} collective-permute-done((bf16[256,256]{1,0:T(8,128)(2,1)S(1)}, bf16[256,256]{1,0:T(8,128)(2,1)S(1)}, u32[]{:S(2)}, u32[]{:S(2)}) %collective-permute-start.3) | collective-permute-done | bytes 131104 | tf_op jit(solution)/shard_map/ppermute | solution.py:410
  49.5 2.7 %collective-permute-done.5.theirs = bf16[4,512,256]{2,1,0:T(8,128)(2,1)} collective-permute-done((bf16[4,512,256]{2,1,0:T(8,128)(2,1)S(1)}, bf16[4,512,256]{2,1,0:T(8,128)(2,1)}, u32[]{:S(2)}, u32[]{:S(2)}) %collective-permute-start.5) | collective-permute-done | bytes 1048608 | tf_op jit(solution)/shard_map/ppermute | solution.py:413
  52.2 19.9 %all-to-all-done = bf16[16,16,4096]{2,1,0:T(8,128)(2,1)} async-done(((bf16[16,16,4096]{2,1,0:T(8,128)(2,1)}), bf16[16,16,4096]{2,1,0:T(8,128)(2,1)}, u32[]{:S(2)}, u32[]{:S(2)}) %all-to-all-start) | async-done | bytes 2097184 | tf_op jit(solution)/shard_map/all_to_all | solution.py:430
  72.0 2.7 %project.1 = bf16[256,256]{1,0:T(8,128)(2,1)S(1)} custom-call(s32[4]{0:T(128)S(1)} %pad_add_fusion.place, bf16[256,4096]{1,0:T(8,128)(2,1)} %bitcast.12.attn, bf16[4,512,256]{2,1,0:T(8,128)(2,1)S(1)} %pad_maximum_fusion.mine, bf16[4,512,256]{2,1,0:T(8,128)(2,1)} %collective-permute-done.5.theirs), custom_call_target="tpu_custom_call" | custom-call | bytes 10800000 | tf_op jit(solution)/shard_map/project/pallas_call | solution.py:164
  76.4 3.4 %collective-permute-done.6 = bf16[256,256]{1,0:T(8,128)(2,1)S(1)} collective-permute-done((bf16[256,256]{1,0:T(8,128)(2,1)S(1)}, bf16[256,256]{1,0:T(8,128)(2,1)S(1)}, u32[]{:S(2)}, u32[]{:S(2)}) %collective-permute-start.6) | collective-permute-done | bytes 131104 | tf_op jit(solution)/shard_map/ppermute | solution.py:435
  84.3 3.2 %collective-permute-start.9 = (f32[1,256]{1,0:T(1,128)S(1)}, f32[1,256]{1,0:T(1,128)S(1)}, u32[]{:S(2)}, u32[]{:S(2)}) collective-permute-start(f32[1,256]{1,0:T(1,128)S(1)} %add.38), channel_id=1, source_target_pairs={{0,4},{2,6},{4,0},{6,2},{8,12},{10,14},{12,8},{14,10},{16,20},{18,... | collective-permute-start | bytes 3080 | tf_op jit(solution)/shard_map/ppermute | solution.py:444
  89.4 1.9 collective-permute-start.12
  93.4 14.4 %all-to-all-start.1 = ((bf16[16,192,256]{2,1,0:T(8,128)(2,1)}), bf16[16,192,256]{2,1,0:T(8,128)(2,1)S(1)}, u32[]{:S(2)}, u32[]{:S(2)}) async-start(bf16[16,192,256]{2,1,0:T(8,128)(2,1)} %copy-done.1), calls=%async_computation.1 | async-start | bytes 3145728 | tf_op jit(solution)/shard_map/all_to_all | solution.py:449
  107.8 1.9 collective-permute-start.10
  109.7 9.4 %collective-permute-done.10 = f32[1,256]{1,0:T(1,128)S(1)} collective-permute-done((f32[1,256]{1,0:T(1,128)S(1)}, f32[1,256]{1,0:T(1,128)S(1)}, u32[]{:S(2)}, u32[]{:S(2)}) %collective-permute-start.10) | collective-permute-done | bytes 1056 | tf_op jit(solution)/shard_map/ppermute | solution.py:452
  119.1 2.7 %collective-permute-start.11 = (f32[1,256]{1,0:T(1,128)S(1)}, f32[1,256]{1,0:T(1,128)S(1)}, u32[]{:S(2)}, u32[]{:S(2)}) collective-permute-start(f32[1,256]{1,0:T(1,128)S(1)} %add.40), channel_id=1, source_target_pairs={{0,16},{2,18},{4,20},{6,22},{8,24},{10,26},{12,28},{14,30},{16,0},... | collective-permute-start | bytes 3080 | tf_op jit(solution)/shard_map/ppermute | solution.py:452
  121.8 4.8 %collective-permute-done.11 = f32[1,256]{1,0:T(1,128)S(1)} collective-permute-done((f32[1,256]{1,0:T(1,128)S(1)}, f32[1,256]{1,0:T(1,128)S(1)}, u32[]{:S(2)}, u32[]{:S(2)}) %collective-permute-start.11) | collective-permute-done | bytes 1056 | tf_op jit(solution)/shard_map/ppermute | solution.py:452
  126.7 5.9 %all-to-all-done.1.arrived = bf16[16,192,256]{2,1,0:T(8,128)(2,1)S(1)} async-done(((bf16[16,192,256]{2,1,0:T(8,128)(2,1)}), bf16[16,192,256]{2,1,0:T(8,128)(2,1)S(1)}, u32[]{:S(2)}, u32[]{:S(2)}) %all-to-all-start.1) | async-done | bytes 1572896 | tf_op jit(solution)/shard_map/all_to_all | solution.py:449
  132.6 2.2 expand_far.1
  135.3 3.7 %collective-permute-start.14 = (bf16[96,1536]{1,0:T(8,128)(2,1)S(1)}, bf16[96,1536]{1,0:T(8,128)(2,1)S(1)}, u32[]{:S(2)}, u32[]{:S(2)}) collective-permute-start(bf16[96,1536]{1,0:T(8,128)(2,1)S(1)} %get-tuple-element.46), channel_id=1, source_target_pairs={{0,192},{32,224},{64,0},{96,32},{128,64},{160,96},{192,128},{224,1... | collective-permute-start | bytes 884744 | tf_op jit(solution)/shard_map/ppermute | solution.py:410
  139.0 4.2 %expand_near.1 = (f32[96,1536]{1,0:T(8,128)S(1)}, bf16[96,1536]{1,0:T(8,128)(2,1)}, bf16[96,1536]{1,0:T(8,128)(2,1)}, f32[96,1536]{1,0:T(8,128)S(1)}, f32[192,1536]{1,0:T(8,128)S(1)}) custom-call(s32[4]{0:T(128)S(1)} %pad_add_fusion.place, bf16[16,192,256]{2,1,0:T(8,128)(2,1)S(1)} %all-to-all-done.1.arrived, bf16[2,256,1536]{2,1,0:T(8,128)(2,1)S(1)} %bitcast.38, ...), custom_call_target="tpu_custom_call" | custom-call | bytes 14400000 | tf_op jit(solution)/shard_map/expand_near/pallas_call | solution.py:247
  144.3 4.1 %collective-permute-start.17 = (bf16[96,1536]{1,0:T(8,128)(2,1)}, bf16[96,1536]{1,0:T(8,128)(2,1)S(1)}, u32[]{:S(2)}, u32[]{:S(2)}) collective-permute-start(bf16[96,1536]{1,0:T(8,128)(2,1)} %get-tuple-element.52), channel_id=1, source_target_pairs={{0,192},{32,224},{64,0},{96,32},{128,64},{160,96},{192,128},{224,1... | collective-permute-start | bytes 884744 | tf_op jit(solution)/shard_map/ppermute | solution.py:410
  148.4 4.8 %collective-permute-done.13 = bf16[96,1536]{1,0:T(8,128)(2,1)S(1)} collective-permute-done((bf16[96,1536]{1,0:T(8,128)(2,1)S(1)}, bf16[96,1536]{1,0:T(8,128)(2,1)S(1)}, u32[]{:S(2)}, u32[]{:S(2)}) %collective-permute-start.13) | collective-permute-done | bytes 294944 | tf_op jit(solution)/shard_map/ppermute | solution.py:410
  156.5 5.3 %collective-permute-done.16.refs_2_ = bf16[96,1536]{1,0:T(8,128)(2,1)S(1)} collective-permute-done((bf16[96,1536]{1,0:T(8,128)(2,1)}, bf16[96,1536]{1,0:T(8,128)(2,1)S(1)}, u32[]{:S(2)}, u32[]{:S(2)}) %collective-permute-start.16) | collective-permute-done | bytes 294944 | tf_op jit(solution)/shard_map/ppermute | solution.py:410
  162.6 5.9 %collective-permute-done.18.refs_4_ = bf16[96,1536]{1,0:T(8,128)(2,1)S(1)} collective-permute-done((bf16[96,1536]{1,0:T(8,128)(2,1)S(1)}, bf16[96,1536]{1,0:T(8,128)(2,1)S(1)}, u32[]{:S(2)}, u32[]{:S(2)}) %collective-permute-start.18) | collective-permute-done | bytes 294944 | tf_op jit(solution)/shard_map/ppermute | solution.py:410
  172.9 6.6 %contract.1 = bf16[16,192,256]{2,1,0:T(8,128)(2,1)} custom-call(s32[4]{0:T(128)S(1)} %pad_add_fusion.place, s32[8,256]{1,0:T(8,128)S(1)} %copy.17.ids, f32[1,256]{1,0:T(1,128)S(1)} %add.41.squares, f32[192,1536]{1,0:T(8,128)S(1)} %copy-done.4, bf16[96,1536]{1,0:T(8,128)(2,1)S(1)} %copy-done.10, bf16[96,1536]{1,0:T(8,128)(2,1)S(1)} %collective-permute-done.16.refs_2_, ...), custom_call_target="tpu_custom_call" | custom-call | bytes 18000000 | tf_op jit(solution)/shard_map/contract/pallas_call | solution.py:325
  179.4 16.2 %all-to-all-start.2 = ((bf16[16,192,256]{2,1,0:T(8,128)(2,1)}), bf16[16,192,256]{2,1,0:T(8,128)(2,1)S(1)}, u32[]{:S(2)}, u32[]{:S(2)}) async-start(bf16[16,192,256]{2,1,0:T(8,128)(2,1)} %contract.1), calls=%async_computation.2 | async-start | bytes 3145728 | tf_op jit(solution)/shard_map/all_to_all | solution.py:474
  195.8 24.6 %all-to-all-done.2.refs_0_ = bf16[16,192,256]{2,1,0:T(8,128)(2,1)S(1)} async-done(((bf16[16,192,256]{2,1,0:T(8,128)(2,1)}), bf16[16,192,256]{2,1,0:T(8,128)(2,1)S(1)}, u32[]{:S(2)}, u32[]{:S(2)}) %all-to-all-start.2) | async-done | bytes 1572896 | tf_op jit(solution)/shard_map/all_to_all | solution.py:474
  220.4 2.0 combine.1
  222.5 5.0 %collective-permute-done.19 = bf16[256,256]{1,0:T(8,128)(2,1)S(1)} collective-permute-done((bf16[256,256]{1,0:T(8,128)(2,1)S(1)}, bf16[256,256]{1,0:T(8,128)(2,1)S(1)}, u32[]{:S(2)}, u32[]{:S(2)}) %collective-permute-start.19) | collective-permute-done | bytes 131104 | tf_op jit(solution)/shard_map/ppermute | solution.py:476
  (102 shorter events, 27.6 us)
Async XLA Ops:
  6.5 163.4 %all-gather.5.cloned.1.call-start = ((), (), s32[]{:S(2)}) async-start(), calls=%async_computation.3 | async-start | bytes 3538944 | tf_op jit(solution)/shard_map/all_gather | solution.py:423
  6.6 18.3 %collective-permute-start.1 = (bf16[512,256]{1,0:T(8,128)(2,1)}, bf16[512,256]{1,0:T(8,128)(2,1)S(1)}, u32[]{:S(2)}, u32[]{:S(2)}) collective-permute-start(bf16[512,256]{1,0:T(8,128)(2,1)} %param.19), channel_id=1, source_target_pairs={{0,64},{32,96},{64,128},{96,160},{128,192},{160,224},{192,0},{224,... | collective-permute-start | bytes 786440 | tf_op jit(solution)/shard_map/ppermute | solution.py:410
  9.9 15.0 %collective-permute-start.2 = (bf16[512,256]{1,0:T(8,128)(2,1)}, bf16[512,256]{1,0:T(8,128)(2,1)S(1)}, u32[]{:S(2)}, u32[]{:S(2)}) collective-permute-start(bf16[512,256]{1,0:T(8,128)(2,1)} %param.19), channel_id=1, source_target_pairs={{0,192},{32,224},{64,0},{96,32},{128,64},{160,96},{192,128},{224,1... | collective-permute-start | bytes 786440 | tf_op jit(solution)/shard_map/ppermute | solution.py:410
  13.0 11.9 %collective-permute-start = (s32[8,256]{0,1:T(8,128)S(1)}, s32[8,256]{0,1:T(8,128)S(1)}, u32[]{:S(2)}, u32[]{:S(2)}) collective-permute-start(s32[8,256]{0,1:T(8,128)S(1)} %bitcast.39), channel_id=1, source_target_pairs={{0,0},{2,2},{4,4},{6,6},{8,64},{10,66},{12,68},{14,70},{16,128},{1... | collective-permute-start | bytes 24584 | tf_op jit(solution)/shard_map/ppermute | solution.py:416
  26.0 14.7 %copy-start.17 = (bf16[512,256]{1,0:T(8,128)(2,1)S(1)}, bf16[512,256]{1,0:T(8,128)(2,1)}, u32[]{:S(2)}) copy-start(bf16[512,256]{1,0:T(8,128)(2,1)} %copy-done.16) | copy-start | bytes 786436
  26.0 17.1 %copy-start.19 = (bf16[512,256]{1,0:T(8,128)(2,1)S(1)}, bf16[512,256]{1,0:T(8,128)(2,1)}, u32[]{:S(2)}) copy-start(bf16[512,256]{1,0:T(8,128)(2,1)} %copy-done.18) | copy-start | bytes 786436
  26.0 23.1 %copy-start.23 = (bf16[512,256]{1,0:T(8,128)(2,1)S(1)}, bf16[512,256]{1,0:T(8,128)(2,1)}, u32[]{:S(2)}) copy-start(bf16[512,256]{1,0:T(8,128)(2,1)} %param.19) | copy-start | bytes 786436
  26.0 46.0 %all-to-all-start = ((bf16[16,16,4096]{2,1,0:T(8,128)(2,1)}), bf16[16,16,4096]{2,1,0:T(8,128)(2,1)}, u32[]{:S(2)}, u32[]{:S(2)}) async-start(bf16[16,16,4096]{2,1,0:T(8,128)(2,1)} %copy-done), calls=%async_computation | async-start | bytes 4194304 | tf_op jit(solution)/shard_map/all_to_all | solution.py:430
  40.6 129.3 %all-gather.7.cloned.1.call-start = ((), (), s32[]{:S(2)}) async-start(), calls=%async_computation.4 | async-start | bytes 3538944 | tf_op jit(solution)/shard_map/all_gather | solution.py:447
  40.7 7.5 %collective-permute-start.3 = (bf16[256,256]{1,0:T(8,128)(2,1)S(1)}, bf16[256,256]{1,0:T(8,128)(2,1)S(1)}, u32[]{:S(2)}, u32[]{:S(2)}) collective-permute-start(bf16[256,256]{1,0:T(8,128)(2,1)S(1)} %slice.13), channel_id=1, source_target_pairs={{0,64},{32,96},{64,128},{96,160},{128,192},{160,224},{192,0},{224,... | collective-permute-start | bytes 393224 | tf_op jit(solution)/shard_map/ppermute | solution.py:410
  43.1 6.0 %collective-permute-start.4 = (bf16[256,256]{1,0:T(8,128)(2,1)S(1)}, bf16[256,256]{1,0:T(8,128)(2,1)S(1)}, u32[]{:S(2)}, u32[]{:S(2)}) collective-permute-start(bf16[256,256]{1,0:T(8,128)(2,1)S(1)} %slice.14), channel_id=1, source_target_pairs={{0,192},{32,224},{64,0},{96,32},{128,64},{160,96},{192,128},{224,1... | collective-permute-start | bytes 393224 | tf_op jit(solution)/shard_map/ppermute | solution.py:410
  49.3 2.9 %collective-permute-start.5 = (bf16[4,512,256]{2,1,0:T(8,128)(2,1)S(1)}, bf16[4,512,256]{2,1,0:T(8,128)(2,1)}, u32[]{:S(2)}, u32[]{:S(2)}) collective-permute-start(bf16[4,512,256]{2,1,0:T(8,128)(2,1)S(1)} %pad_maximum_fusion.mine), channel_id=1, source_target_pairs={{0,32},{32,0},{64,96},{96,64},{128,160},{160,128},{192,224},{224,1... | collective-permute-start | bytes 3145736 | tf_op jit(solution)/shard_map/ppermute | solution.py:413
  72.0 19.4 %copy-start.25 = (s32[8,256]{0,1:T(8,128)S(1)}, s32[8,256]{0,1:T(8,128)}, u32[]{:S(2)}) copy-start(s32[8,256]{0,1:T(8,128)} %copy-done.24) | copy-start | bytes 24580
  74.8 5.1 %collective-permute-start.6 = (bf16[256,256]{1,0:T(8,128)(2,1)S(1)}, bf16[256,256]{1,0:T(8,128)(2,1)S(1)}, u32[]{:S(2)}, u32[]{:S(2)}) collective-permute-start(bf16[256,256]{1,0:T(8,128)(2,1)S(1)} %project.1), channel_id=1, source_target_pairs={{0,1},{1,0},{2,3},{3,2},{4,5},{5,4},{6,7},{7,6},{8,9},{9,8},{10,11... | collective-permute-start | bytes 393224 | tf_op jit(solution)/shard_map/ppermute | solution.py:435
  80.0 9.4 %collective-permute-start.7 = (bf16[256,256]{1,0:T(8,128)(2,1)S(1)}, bf16[256,256]{1,0:T(8,128)(2,1)S(1)}, u32[]{:S(2)}, u32[]{:S(2)}) collective-permute-start(bf16[256,256]{1,0:T(8,128)(2,1)S(1)} %get-tuple-element.60), channel_id=1, source_target_pairs={{0,0},{2,2},{4,4},{6,6},{8,64},{10,66},{12,68},{14,70},{16,128},{1... | collective-permute-start | bytes 393224 | tf_op jit(solution)/shard_map/ppermute | solution.py:440
  80.7 3.7 %collective-permute-start.8 = (f32[1,256]{1,0:T(1,128)S(1)}, f32[1,256]{1,0:T(1,128)S(1)}, u32[]{:S(2)}, u32[]{:S(2)}) collective-permute-start(f32[1,256]{1,0:T(1,128)S(1)} %bitcast.49), channel_id=1, source_target_pairs={{0,2},{2,0},{4,6},{6,4},{8,10},{10,8},{12,14},{14,12},{16,18},{18,... | collective-permute-start | bytes 3080 | tf_op jit(solution)/shard_map/ppermute | solution.py:444
  84.3 5.1 %collective-permute-start.9 = (f32[1,256]{1,0:T(1,128)S(1)}, f32[1,256]{1,0:T(1,128)S(1)}, u32[]{:S(2)}, u32[]{:S(2)}) collective-permute-start(f32[1,256]{1,0:T(1,128)S(1)} %add.38), channel_id=1, source_target_pairs={{0,4},{2,6},{4,0},{6,2},{8,12},{10,14},{12,8},{14,10},{16,20},{18,... | collective-permute-start | bytes 3080 | tf_op jit(solution)/shard_map/ppermute | solution.py:444
  89.4 43.2 %collective-permute-start.12 = (bf16[512,1536]{1,0:T(8,128)(2,1)S(1)}, bf16[512,1536]{1,0:T(8,128)(2,1)}, u32[]{:S(2)}, u32[]{:S(2)}) collective-permute-start(bf16[512,1536]{1,0:T(8,128)(2,1)S(1)} %bitcast.36), channel_id=1, source_target_pairs={{0,32},{32,0},{64,96},{96,64},{128,160},{160,128},{192,224},{224,1... | collective-permute-start | bytes 4718600 | tf_op jit(solution)/shard_map/ppermute | solution.py:413
  93.4 39.2 %all-to-all-start.1 = ((bf16[16,192,256]{2,1,0:T(8,128)(2,1)}), bf16[16,192,256]{2,1,0:T(8,128)(2,1)S(1)}, u32[]{:S(2)}, u32[]{:S(2)}) async-start(bf16[16,192,256]{2,1,0:T(8,128)(2,1)} %copy-done.1), calls=%async_computation.1 | async-start | bytes 3145728 | tf_op jit(solution)/shard_map/all_to_all | solution.py:449
  107.8 11.3 %collective-permute-start.10 = (f32[1,256]{1,0:T(1,128)S(1)}, f32[1,256]{1,0:T(1,128)S(1)}, u32[]{:S(2)}, u32[]{:S(2)}) collective-permute-start(f32[1,256]{1,0:T(1,128)S(1)} %add.39), channel_id=1, source_target_pairs={{0,8},{2,10},{4,12},{6,14},{8,0},{10,2},{12,4},{14,6},{16,24},{18,... | collective-permute-start | bytes 3080 | tf_op jit(solution)/shard_map/ppermute | solution.py:452
  119.1 7.5 %collective-permute-start.11 = (f32[1,256]{1,0:T(1,128)S(1)}, f32[1,256]{1,0:T(1,128)S(1)}, u32[]{:S(2)}, u32[]{:S(2)}) collective-permute-start(f32[1,256]{1,0:T(1,128)S(1)} %add.40), channel_id=1, source_target_pairs={{0,16},{2,18},{4,20},{6,22},{8,24},{10,26},{12,28},{14,30},{16,0},... | collective-permute-start | bytes 3080 | tf_op jit(solution)/shard_map/ppermute | solution.py:452
  134.8 18.4 %collective-permute-start.13 = (bf16[96,1536]{1,0:T(8,128)(2,1)S(1)}, bf16[96,1536]{1,0:T(8,128)(2,1)S(1)}, u32[]{:S(2)}, u32[]{:S(2)}) collective-permute-start(bf16[96,1536]{1,0:T(8,128)(2,1)S(1)} %get-tuple-element.45), channel_id=1, source_target_pairs={{0,64},{32,96},{64,128},{96,160},{128,192},{160,224},{192,0},{224,... | collective-permute-start | bytes 884744 | tf_op jit(solution)/shard_map/ppermute | solution.py:410
  135.3 17.9 %collective-permute-start.14 = (bf16[96,1536]{1,0:T(8,128)(2,1)S(1)}, bf16[96,1536]{1,0:T(8,128)(2,1)S(1)}, u32[]{:S(2)}, u32[]{:S(2)}) collective-permute-start(bf16[96,1536]{1,0:T(8,128)(2,1)S(1)} %get-tuple-element.46), channel_id=1, source_target_pairs={{0,192},{32,224},{64,0},{96,32},{128,64},{160,96},{192,128},{224,1... | collective-permute-start | bytes 884744 | tf_op jit(solution)/shard_map/ppermute | solution.py:410
  144.3 25.7 %copy-start.4 = (f32[192,1536]{1,0:T(8,128)S(1)}, f32[192,1536]{1,0:T(8,128)}, u32[]{:S(2)}) copy-start(f32[192,1536]{1,0:T(8,128)} %copy-done.3) | copy-start | bytes 3538948
  144.3 17.5 %collective-permute-start.16 = (bf16[96,1536]{1,0:T(8,128)(2,1)}, bf16[96,1536]{1,0:T(8,128)(2,1)S(1)}, u32[]{:S(2)}, u32[]{:S(2)}) collective-permute-start(bf16[96,1536]{1,0:T(8,128)(2,1)} %get-tuple-element.51), channel_id=1, source_target_pairs={{0,64},{32,96},{64,128},{96,160},{128,192},{160,224},{192,0},{224,... | collective-permute-start | bytes 884744 | tf_op jit(solution)/shard_map/ppermute | solution.py:410
  144.3 17.5 %collective-permute-start.17 = (bf16[96,1536]{1,0:T(8,128)(2,1)}, bf16[96,1536]{1,0:T(8,128)(2,1)S(1)}, u32[]{:S(2)}, u32[]{:S(2)}) collective-permute-start(bf16[96,1536]{1,0:T(8,128)(2,1)} %get-tuple-element.52), channel_id=1, source_target_pairs={{0,192},{32,224},{64,0},{96,32},{128,64},{160,96},{192,128},{224,1... | collective-permute-start | bytes 884744 | tf_op jit(solution)/shard_map/ppermute | solution.py:410
  153.3 15.2 %collective-permute-start.18 = (bf16[96,1536]{1,0:T(8,128)(2,1)S(1)}, bf16[96,1536]{1,0:T(8,128)(2,1)S(1)}, u32[]{:S(2)}, u32[]{:S(2)}) collective-permute-start(bf16[96,1536]{1,0:T(8,128)(2,1)S(1)} %add_convert_fusion), channel_id=1, source_target_pairs={{0,192},{32,224},{64,0},{96,32},{128,64},{160,96},{192,128},{224,1... | collective-permute-start | bytes 884744 | tf_op jit(solution)/shard_map/ppermute | solution.py:410
  155.2 14.0 %collective-permute-start.15 = (bf16[96,1536]{1,0:T(8,128)(2,1)S(1)}, bf16[96,1536]{1,0:T(8,128)(2,1)S(1)}, u32[]{:S(2)}, u32[]{:S(2)}) collective-permute-start(bf16[96,1536]{1,0:T(8,128)(2,1)S(1)} %add_convert_fusion.1), channel_id=1, source_target_pairs={{0,64},{32,96},{64,128},{96,160},{128,192},{160,224},{192,0},{224,... | collective-permute-start | bytes 884744 | tf_op jit(solution)/shard_map/ppermute | solution.py:410
  179.4 16.2 %copy-start.26 = (bf16[4,64,8]{1,2,0:T(8,128)(2,1)S(1)}, bf16[4,64,8]{1,2,0:T(8,128)(2,1)}, u32[]{:S(2)}) copy-start(bf16[4,64,8]{1,2,0:T(8,128)(2,1)} %param.23) | copy-start | bytes 12292
  179.4 40.9 %all-to-all-start.2 = ((bf16[16,192,256]{2,1,0:T(8,128)(2,1)}), bf16[16,192,256]{2,1,0:T(8,128)(2,1)S(1)}, u32[]{:S(2)}, u32[]{:S(2)}) async-start(bf16[16,192,256]{2,1,0:T(8,128)(2,1)} %contract.1), calls=%async_computation.2 | async-start | bytes 3145728 | tf_op jit(solution)/shard_map/all_to_all | solution.py:474
  195.7 31.8 %copy-start.22 = (bf16[256,256]{1,0:T(8,128)(2,1)S(1)}, bf16[256,256]{1,0:T(8,128)(2,1)}, u32[]{:S(2)}) copy-start(bf16[256,256]{1,0:T(8,128)(2,1)} %copy-done.21) | copy-start | bytes 393220
  222.4 5.1 %collective-permute-start.19 = (bf16[256,256]{1,0:T(8,128)(2,1)S(1)}, bf16[256,256]{1,0:T(8,128)(2,1)S(1)}, u32[]{:S(2)}, u32[]{:S(2)}) collective-permute-start(bf16[256,256]{1,0:T(8,128)(2,1)S(1)} %combine.1), channel_id=1, source_target_pairs={{0,1},{1,0},{2,3},{3,2},{4,5},{5,4},{6,7},{7,6},{8,9},{9,8},{10,11... | collective-permute-start | bytes 393224 | tf_op jit(solution)/shard_map/ppermute | solution.py:476
  (21 other events, 82.8 us)
Sparse Core Ops, SparseCore 0:
  25.1 54.9 all-gather.4
  89.6 48.0 all-gather.6
